TPU v7x, 32 devices: a whole 2x2x4 slice. The times are simulated.
32 devices in a mesh: rows: 8 (over z, x), cols: 4 (over y, core).
Axes of the slice: x: 2, y: 2, z: 4, core: 2. Of those that a mesh axis runs over, the one named last changes fastest.
Arguments:
- hidden_acts: bfloat16 [1, 27648, 2560], P(None, 'rows'), may hold values from -17 to 17
- out_grads: bfloat16 [1, 2560, 5120], P(None, None, 'cols'), may hold values from -13 to 13
- row_signs: int32 [27648], P('rows'), may hold values from -1 to 1, as said below
- kept_index: int32 [16384], P('rows'), may hold values from 0 to 32767, as said below
Outputs:
- sketch: float32 [1, 16384, 5120], P(None, 'rows', 'cols')
Inputs may be any that keep to these rules, and one draw needn't show every extreme that they name: `row_signs`: each entry is +1 or -1. `kept_index`: for each b and each s = 0 .. 7, entries b * 2048 + s * 256 to b * 2048 + (s + 1) * 256 - 1 are distinct padded rows within b * 4096 + s * 512 to b * 4096 + (s + 1) * 512 - 1.
All inputs are finite; a program needn't handle non-finite values.
Results may differ from a plain program's by a relative error of at most 0.0003.
Values sent between devices are 32-bit elements; how exact they have to be, the bound alone decides.
A program may use at most 128 MiB of HBM per device.

v0:
```python
import jax
import jax.numpy as jnp
from jax import lax
from jax.sharding import PartitionSpec as P

D = 5120
PADDED = 32768


epsilon = 1e-06


def partner_2(value, axis, bit):
    mask = 2**bit
    pairs = [(source, source ^ mask) for source in range(lax.axis_size(axis))]
    return lax.ppermute(value, axis, pairs)


def sylvester(length):
    indices = jnp.arange(length, dtype=jnp.int32)
    intersection = indices[:, None] & indices[None, :]
    parity = jnp.zeros_like(intersection)
    for bit_level in range(length.bit_length() - 1):
        parity = parity ^ intersection >> bit_level & 1
    return 1 - 2 * parity


def mix_kept(block_mixed, kept_index, pad_rows):
    row_devices = lax.axis_size("rows")
    position = lax.axis_index("rows")
    mixed_rows = block_mixed
    for bit_level in range(row_devices.bit_length() - 1):
        partner = partner_2(mixed_rows, "rows", bit_level)
        upper_half = position >> bit_level & 1 == 1
        mixed_rows = jnp.where(upper_half, partner - mixed_rows, mixed_rows + partner)
    return jnp.take(mixed_rows, kept_index - position * pad_rows, axis=1)


def local(hidden_acts, out_grads, row_signs, kept_index):
    row_devices = lax.axis_size("rows")
    pad_rows = PADDED // row_devices
    own_rows = hidden_acts.shape[1]
    gradient = jnp.einsum(
        "erl,elc->erc", hidden_acts, out_grads, preferred_element_type=jnp.float32
    )
    local_squares = jnp.sum(gradient * gradient, axis=(1, 2))
    squares_all = lax.psum(local_squares, ("rows", "cols"))
    token_share = hidden_acts.shape[2] // lax.axis_size("cols")
    acts_slice = lax.dynamic_slice_in_dim(
        hidden_acts, lax.axis_index("cols") * token_share, token_share, 2
    )
    signed_acts = acts_slice * row_signs.astype(jnp.bfloat16)[None, :, None]
    padded = jnp.pad(signed_acts, ((0, 0), (0, pad_rows - own_rows), (0, 0)))
    inner_table = sylvester(pad_rows).astype(jnp.bfloat16)
    block_mixed = jnp.einsum("ij,ejt->eit", inner_table, padded, preferred_element_type=jnp.float32)
    kept_acts = mix_kept(block_mixed, kept_index, pad_rows)
    grads_piece = out_grads.astype(jnp.float32)
    picked = jnp.einsum(
        "ekt,etc->ekc",
        lax.all_gather(kept_acts, "cols", axis=2, tiled=True),
        grads_piece,
        precision=lax.Precision.HIGHEST,
    )
    inv_norm = lax.rsqrt(squares_all / D + epsilon)
    return picked * inv_norm[:, None, None]


def solution(mesh):
    return jax.shard_map(
        local,
        mesh=mesh,
        in_specs=(P(None, "rows", None), P(None, None, "cols"), P("rows"), P("rows")),
        out_specs=P(None, "rows", "cols"),
        check_vma=False,
    )
```

profile of v0, /device:TPU:0, one launch (start us, length us, event | category | flops | bytes accessed | tf_op | source)
XLA Modules:
  0.0 1272.7 jit_solution(9883164457813581069)
XLA Ops:
  6.5 0.0 all-gather.2.cloned.1.call-start
  6.5 0.7 convert_element_type.9
  7.3 3.4 dynamic-slice_multiply_fusion
  10.7 0.4 fusion.33
  11.1 92.6 %fusion.6 = f32[1,4096,640]{1,2,0:T(8,128)} fusion(bf16[4096,640]{1,0:T(8,128)(2,1)S(1)} %fusion.33), kind=kOutput, calls=%fused_computation.11 | convolution fusion | flops 22129147904 | bytes 15728640 | tf_op jit(solution)/shard_map/ij,ejt->eit/dot_general | solution.py:55
  103.7 2.9 collective-permute-start
  106.6 225.7 %collective-permute-done = f32[1,4096,640]{1,2,0:T(8,128)} collective-permute-done((f32[1,4096,640]{1,2,0:T(8,128)}, f32[1,4096,640]{1,2,0:T(8,128)}, u32[]{:S(2)}, u32[]{:S(2)}) %collective-permute-start) | collective-permute-done | bytes 10485792 | tf_op jit(solution)/shard_map/ppermute | solution.py:16
  332.3 14.4 %add_select_fusion.1 = f32[1,4096,640]{1,2,0:T(8,128)} fusion(f32[1,4096,640]{1,2,0:T(8,128)} %fusion.6, f32[1,4096,640]{1,2,0:T(8,128)} %collective-permute-done, pred[]{:T(512)S(6)} %eq.11), kind=kLoop, calls=%fused_computation.10 | loop fusion | flops 7864320 | bytes 31457280 | tf_op jit(solution)/shard_map/jit(_where)/select_n | solution.py:35
  346.7 0.0 copy-start
  346.7 1.8 collective-permute-start.1
  348.5 225.1 %collective-permute-done.1 = f32[1,4096,640]{1,2,0:T(8,128)} collective-permute-done((f32[1,4096,640]{1,2,0:T(8,128)}, f32[1,4096,640]{1,2,0:T(8,128)}, u32[]{:S(2)}, u32[]{:S(2)}) %collective-permute-start.1) | collective-permute-done | bytes 10485792 | tf_op jit(solution)/shard_map/ppermute | solution.py:16
  573.6 14.4 %add_select_fusion = f32[1,4096,640]{1,2,0:T(8,128)} fusion(f32[1,4096,640]{1,2,0:T(8,128)} %add_select_fusion.1, f32[1,4096,640]{1,2,0:T(8,128)} %collective-permute-done.1, pred[]{:T(512)S(6)} %eq.10), kind=kLoop, calls=%fused_computation.9 | loop fusion | flops 7864320 | bytes 31457280 | tf_op jit(solution)/shard_map/jit(_where)/select_n | solution.py:35
  588.0 2.5 collective-permute-start.2
  590.5 0.0 copy-done
  590.5 449.0 %collective-permute-done.2 = f32[1,4096,640]{1,2,0:T(8,128)} collective-permute-done((f32[1,4096,640]{1,2,0:T(8,128)}, f32[1,4096,640]{1,2,0:T(8,128)}, u32[]{:S(2)}, u32[]{:S(2)}) %collective-permute-start.2) | collective-permute-done | bytes 10485792 | tf_op jit(solution)/shard_map/ppermute | solution.py:16
  1039.6 14.4 %select_bitcast_fusion = f32[4096,640]{0,1:T(8,128)} fusion(f32[1,4096,640]{1,2,0:T(8,128)} %add_select_fusion, f32[1,4096,640]{1,2,0:T(8,128)} %collective-permute-done.2, pred[]{:T(512)S(6)} %eq.9), kind=kLoop, calls=%fused_computation.8 | loop fusion | flops 7864320 | bytes 31457280 | tf_op jit(solution)/shard_map/jit(_where)/select_n | solution.py:35
  1054.0 11.3 copy.5
  1065.3 13.9 %gather_fusion = f32[2048,640]{1,0:T(8,128)} fusion(f32[4096,640]{1,0:T(8,128)} %copy.5, s32[2048]{0:T(1024)S(1)} %fusion.16), kind=kCustom, calls=%fused_computation | custom fusion | bytes 10493952 | tf_op jit(solution)/shard_map/jit(_take)/gather | solution.py:36
  1079.1 4.3 bitcast_select_fusion
  1083.5 0.0 all-gather.2.cloned.1.call-update
  1083.5 29.2 %fusion.11 = f32[]{:T(128)} fusion(bf16[1,2560,1280]{2,1,0:T(8,128)(2,1)} %param.5, bf16[1,3456,2560]{2,1,0:T(8,128)(2,1)} %param.4), kind=kOutput, calls=%fused_computation.18 | convolution fusion | flops 22658088960 | bytes 24248324 | tf_op jit(solution)/shard_map/erl,elc->erc/dot_general | solution.py:43
  1112.7 40.3 %psum.7 = f32[1]{0:T(128)} all-reduce(f32[1]{0:T(128)} %bitcast.9), channel_id=1, replica_groups=mesh['rows'=8,'cols'=4] {'rows','cols'}, use_global_device_ids=true, to_apply=%region_1.0 | all-reduce | flops 1 | bytes 8 | tf_op jit(solution)/shard_map/psum | solution.py:47
  1153.7 63.7 %all-gather.2.cloned.1.call-done = f32[1,2048,2560]{2,1,0:T(8,128)} async-done(((f32[1,2048,640]{2,1,0:T(8,128)}), f32[1,2048,2560]{2,1,0:T(8,128)}) %all-gather.2.cloned.1.call-update) | async-done | bytes 20971536 | tf_op jit(solution)/shard_map/all_gather | solution.py:60
  1217.4 48.5 %multiply_bitcast_fusion = f32[1,2048,1280]{2,1,0:T(8,128)} fusion(f32[1,2048,2560]{2,1,0:T(8,128)} %all-gather.2.cloned.1.call-done, bf16[1,2560,1280]{2,1,0:T(8,128)(2,1)} %param.5, f32[]{:T(128)} %bitcast.10), kind=kOutput, calls=%fused_computation.7 | convolution fusion | flops 80533258240 | bytes 38010884 | tf_op jit(solution)/shard_map/ekt,etc->ekc/dot_general | solution.py:58
  (2 shorter events, 0.0 us)
Async XLA Ops:
  6.5 1210.9 %all-gather.2.cloned.1.call-start = ((), (), s32[]{:S(2)}) async-start(), calls=%async_computation | async-start | bytes 26214400 | tf_op jit(solution)/shard_map/all_gather | solution.py:60
  103.7 228.6 %collective-permute-start = (f32[1,4096,640]{1,2,0:T(8,128)}, f32[1,4096,640]{1,2,0:T(8,128)}, u32[]{:S(2)}, u32[]{:S(2)}) collective-permute-start(f32[1,4096,640]{1,2,0:T(8,128)} %fusion.6), channel_id=1, source_target_pairs={{0,4},{4,0},{8,12},{12,8},{16,20},{20,16},{24,28},{28,24},{1,5},{5... | collective-permute-start | bytes 31457288 | tf_op jit(solution)/shard_map/ppermute | solution.py:16
  346.7 243.8 %copy-start = (s32[2048]{0:T(1024)S(1)}, s32[2048]{0:T(1024)}, u32[]{:S(2)}) copy-start(s32[2048]{0:T(1024)} %param.7) | copy-start | bytes 24580
  346.7 226.9 %collective-permute-start.1 = (f32[1,4096,640]{1,2,0:T(8,128)}, f32[1,4096,640]{1,2,0:T(8,128)}, u32[]{:S(2)}, u32[]{:S(2)}) collective-permute-start(f32[1,4096,640]{1,2,0:T(8,128)} %add_select_fusion.1), channel_id=1, source_target_pairs={{0,8},{4,12},{8,0},{12,4},{16,24},{20,28},{24,16},{28,20},{1,9},{5... | collective-permute-start | bytes 31457288 | tf_op jit(solution)/shard_map/ppermute | solution.py:16
  588.0 451.6 %collective-permute-start.2 = (f32[1,4096,640]{1,2,0:T(8,128)}, f32[1,4096,640]{1,2,0:T(8,128)}, u32[]{:S(2)}, u32[]{:S(2)}) collective-permute-start(f32[1,4096,640]{1,2,0:T(8,128)} %add_select_fusion), channel_id=1, source_target_pairs={{0,16},{4,20},{8,24},{12,28},{16,0},{20,4},{24,8},{28,12},{1,17},{... | collective-permute-start | bytes 31457288 | tf_op jit(solution)/shard_map/ppermute | solution.py:16
Sparse Core Ops, SparseCore 0:
  1083.6 133.7 all-gather.1
where the time goes:
time: 1270 us
  waiting for transfers between devices  964 us (76%)
  matrix products  170 us (13%)
  other arithmetic  51.7 us (4%)
  blocking collectives  40.3 us (3%)
  local copies, waits for them, and re-layouts  25.6 us (2%)
  between operations  14.1 us (1%)
    ppermute x3, waiting for transfers between devices, partner_2(): return lax.ppermute(value, axis, pairs)  900 us
    dot_general x1, matrix products, local(): jnp.einsum('ij,ejt->eit', inner_table, padded, preferred_element_type=jnp...  92.6 us
    all_gather x1, waiting for transfers between devices, local(): lax.all_gather(kept_acts, 'cols', axis=2, tiled=True)  63.7 us
    dot_general x1, matrix products, local(): jnp.einsum('ekt,etc->ekc', lax.all_gather(kept_acts, 'cols', axis=2, tile...  48.5 us
    select_n x3, other arithmetic, mix_kept(): jnp.where(upper_half, partner - mixed_rows, mixed_rows + partner)  43.2 us
    psum x1, blocking collectives, local(): squares_all = lax.psum(local_squares, ('rows', 'cols'))  40.3 us
    dot_general x1, matrix products, local(): jnp.einsum('erl,elc->erc', hidden_acts, out_grads, preferred_element_type...  29.2 us
  transfers between devices with their start and end apart: 4, of which 4 were waited for; matrix products, arithmetic and copies ran while one was open for 2% of the time, Pallas kernels for 0%

commit v1 on v0

v1 whole, which is shorter than its diff:
```python
import functools

import jax
import jax.numpy as jnp
from jax import lax
from jax.experimental import pallas as pl
from jax.experimental.pallas import tpu as pltpu
from jax.sharding import PartitionSpec as P

D = 5120
PADDED = 32768
LANES = 128

epsilon = 1e-06


def exchange(value, axis, mask):
    pairs = [(source, source ^ mask) for source in range(lax.axis_size(axis))]
    return lax.ppermute(value, axis, pairs)


def split(value):
    high = lax.reduce_precision(value, 8, 7)
    return high.astype(jnp.bfloat16), (value - high).astype(jnp.bfloat16)


def mix_segments(block, segments):
    rows, tokens = block.shape
    parts = [block.reshape(segments, rows // segments, tokens)[s] for s in range(segments)]
    return jnp.stack(butterfly(parts))


def butterfly(parts):
    segments = len(parts)
    step = 1
    while step < segments:
        parts = [
            parts[s ^ step] - parts[s] if s & step else parts[s] + parts[s ^ step]
            for s in range(segments)
        ]
        step *= 2
    return parts


def table(kept, length):
    column = jnp.arange(length, dtype=jnp.int32)
    parity = lax.population_count((kept & (length - 1))[..., None] & column) & 1
    return (1 - 2 * parity).astype(jnp.bfloat16)


def pick(tables, mixed):
    product = lambda part: jnp.einsum(
        "skj,sjt->skt", tables, part, preferred_element_type=jnp.float32
    )
    high, low = split(mixed)
    return product(high) + product(low)


def operands(own, outer, side, inner):
    flipped = side * own
    return (
        side * outer + own,
        outer - flipped,
        jnp.where(inner, side * outer - own, own),
        flipped,
    )


def pick_kernel(segments, flags_ref, own_ref, outer_ref, table_ref, far_ref, here_ref, near_ref, padded, halves):
    own_rows, tokens = own_ref.shape
    length = padded.shape[1] // segments
    rows = min(length, 32)
    padded[0, :own_rows] = own_ref[...]
    padded[1, :own_rows] = outer_ref[...]
    if own_rows < padded.shape[1]:
        rest = jnp.zeros((padded.shape[1] - own_rows, tokens), jnp.float32)
        padded[0, own_rows:] = rest
        padded[1, own_rows:] = rest
    side = flags_ref[0]
    inner = flags_ref[1]

    @pl.loop(0, length // rows)
    def _(step):
        start = pl.multiple_of(step * rows, rows)
        mixed = [
            butterfly([padded[i, pl.ds(s * length + start, rows), :] for s in range(segments)])
            for i in range(2)
        ]
        for s in range(segments):
            own, outer = mixed[0][s], mixed[1][s]
            flipped = side * own
            here = inner * (side * outer) + (1.0 - 2.0 * inner) * own
            for k, value in enumerate((side * outer + own, outer - flipped, here, flipped)):
                high = value.astype(jnp.bfloat16)
                halves[k, s, pl.ds(start, rows), :tokens] = high
                halves[k, s, pl.ds(start, rows), tokens:] = (
                    value - high.astype(jnp.float32)
                ).astype(jnp.bfloat16)

    @pl.loop(0, segments)
    def _(s):
        for k, out in enumerate((far_ref.at[0], far_ref.at[1], here_ref, near_ref)):
            both = jnp.dot(table_ref[k, s], halves[k, s], preferred_element_type=jnp.float32)
            out[s] = both[:, :tokens] + both[:, tokens:]


def pick_all(tables, own, outer, side, inner, pad_rows):
    _, segments, kept, length = tables.shape
    own_rows, tokens = own.shape
    if length % 32 or kept % 16 or segments > 8:
        padding = ((0, pad_rows - own_rows), (0, 0))
        mixed = mix_segments(jnp.pad(own, padding), segments)
        mixed_outer = mix_segments(jnp.pad(outer, padding), segments)
        found = [pick(t, v) for t, v in zip(tables, operands(mixed, mixed_outer, side, inner))]
        return jnp.stack(found[:2]), found[2], found[3]
    flags = jnp.stack([side, inner.astype(jnp.float32)])
    vmem = pl.BlockSpec(memory_space=pltpu.VMEM)
    shape = lambda *lead: jax.ShapeDtypeStruct((*lead, segments, kept, tokens), jnp.float32)
    return pl.pallas_call(
        functools.partial(pick_kernel, segments),
        out_shape=(shape(2), shape(), shape()),
        in_specs=[pl.BlockSpec(memory_space=pltpu.SMEM), vmem, vmem, vmem],
        out_specs=(vmem, vmem, vmem),
        scratch_shapes=[
            pltpu.VMEM((2, pad_rows, tokens), jnp.float32),
            pltpu.VMEM((4, segments, length, 2 * tokens), jnp.bfloat16),
        ],
        compiler_params=pltpu.CompilerParams(vmem_limit_bytes=40 * 2**20),
        cost_estimate=pl.CostEstimate(
            flops=16 * segments * kept * length * tokens,
            bytes_accessed=2 * tables.size + 8 * own.size + 16 * segments * kept * tokens,
            transcendentals=0,
        ),
    )(flags, own, outer, tables)


def add_kernel(slots, first, last, places_ref, *refs):
    kept_refs, grads_refs = refs[:slots], refs[slots : 2 * slots]
    out_ref = refs[-1]
    kept = [ref[...] for ref in kept_refs]
    high = [value.astype(jnp.bfloat16) for value in kept]
    low = [(v - h.astype(jnp.float32)).astype(jnp.bfloat16) for v, h in zip(kept, high)]
    grads = jnp.concatenate([ref[...] for ref in grads_refs], axis=0)
    total = jnp.dot(jnp.concatenate(high, axis=1), grads, preferred_element_type=jnp.float32)
    total += jnp.dot(jnp.concatenate(low, axis=1), grads, preferred_element_type=jnp.float32)
    if not first:
        total += refs[2 * slots][...]
    if last:
        total *= refs[2 * slots + (0 if first else 1)][0]
    out_ref[...] = total


def add_products(total, kept, out_grads, places, scale):
    slots = len(kept)
    keep, chunk = kept[0].shape
    width = out_grads.shape[1]
    tile = min(256, keep)
    slab = pl.BlockSpec((tile, width), lambda i, places: (i, 0))
    grads_spec = lambda slot: pl.BlockSpec((chunk, width), lambda i, places: (places[slot], 0))
    in_specs = [pl.BlockSpec((tile, chunk), lambda i, places: (i, 0))] * slots
    in_specs += [grads_spec(slot) for slot in range(slots)]
    operands_ = list(kept) + [out_grads] * slots
    aliases = {}
    if total is not None:
        aliases = {1 + len(operands_): 0}
        in_specs.append(slab)
        operands_.append(total)
    if scale is not None:
        in_specs.append(pl.BlockSpec(memory_space=pltpu.SMEM))
        operands_.append(scale.reshape(1))
    return pl.pallas_call(
        functools.partial(add_kernel, slots, total is None, scale is not None),
        out_shape=jax.ShapeDtypeStruct((keep, width), jnp.float32),
        grid_spec=pltpu.PrefetchScalarGridSpec(
            num_scalar_prefetch=1,
            grid=(keep // tile,),
            in_specs=in_specs,
            out_specs=slab,
        ),
        input_output_aliases=aliases,
        compiler_params=pltpu.CompilerParams(vmem_limit_bytes=40 * 2**20),
        cost_estimate=pl.CostEstimate(
            flops=4 * slots * keep * chunk * width,
            bytes_accessed=8 * keep * width + 4 * slots * keep * chunk,
            transcendentals=0,
        ),
    )(places, *operands_)


def after(value, earlier):
    if earlier is None:
        return value
    return lax.optimization_barrier((value, earlier))[0]


def local(hidden_acts, out_grads, row_signs, kept_index):
    row_devices = lax.axis_size("rows")
    col_devices = lax.axis_size("cols")
    pad_rows = PADDED // row_devices
    examples, own_rows, tokens = hidden_acts.shape
    keep = kept_index.shape[0]
    length = pad_rows // row_devices
    position = lax.axis_index("rows")
    column = lax.axis_index("cols")
    low = row_devices // 4
    line = position // low
    offset = position % low
    inner = (line == 1) | (line == 2)
    left = line < 2

    kept_all = lax.all_gather(kept_index, "rows", axis=0)

    def kept_of(group):
        whole = lax.dynamic_index_in_dim(kept_all, group * low + offset, 0, keepdims=False)
        return whole.reshape(row_devices, keep // row_devices)

    own_kept = kept_index.reshape(row_devices, keep // row_devices)
    tables = table(
        jnp.stack(
            [
                kept_of(jnp.where(left, 2, 1)),
                kept_of(jnp.where(left, 3, 0)),
                own_kept,
                kept_of(jnp.where(left, 0, 3)),
            ]
        ),
        length,
    )

    line_pairs = lambda pairs: [(s * low + o, d * low + o) for s, d in pairs for o in range(low)]
    to_inner = line_pairs([(0, 1), (3, 2)])
    across = line_pairs([(1, 2), (2, 1)])
    to_outer = line_pairs([(1, 0), (2, 3)])

    share = tokens // col_devices
    chunk = min(LANES, share)
    signs = row_signs.astype(jnp.float32)[:, None]
    side = jnp.where(left, 1.0, -1.0).astype(jnp.float32)
    block = share // chunk
    results = []
    for example in range(examples):
        grads = out_grads[example]
        gradient = jnp.dot(hidden_acts[example], grads, preferred_element_type=jnp.float32)
        squares = lax.psum(jnp.sum(gradient * gradient), ("rows", "cols"))
        inv_norm = lax.rsqrt(squares / D + epsilon)
        total = None
        done = {}

        def send(value, name, move):
            arrived = move(after(value, done.get(name)))
            done[name] = arrived
            return arrived

        for number in range(block):
            acts = lax.dynamic_slice_in_dim(
                hidden_acts[example], column * share + number * chunk, chunk, 1
            )
            own = acts.astype(jnp.float32) * signs
            mask = 1
            while mask < low:
                other = send(own, ("mix", mask), lambda v: exchange(v, "rows", mask))
                own = jnp.where((position & mask) != 0, other - own, own + other)
                mask *= 2
            outer = send(own, "inner", lambda v: lax.ppermute(v, "rows", to_inner))
            far, here, near = pick_all(tables, own, outer, side, inner, pad_rows)
            arrived = send(far, "across", lambda v: lax.ppermute(v, "rows", across))
            last = send(
                arrived[1] + near, "outer", lambda v: lax.ppermute(v, "rows", to_outer)
            )
            kept = here + jnp.where(inner, arrived[0], last)
            slots = [kept.reshape(keep, chunk)]
            order = [0]
            mask = col_devices // 2
            while mask:
                slots += [
                    send(v, ("cols", mask), lambda v: exchange(v, "cols", mask)) for v in slots
                ]
                order += [slot ^ mask for slot in order]
                mask //= 2
            places = jnp.stack([(column ^ slot) * block + number for slot in order])
            scale = inv_norm if number == block - 1 else None
            total = add_products(total, slots, grads, places, scale)
        results.append(total)
    return jnp.stack(results)


def solution(mesh):
    return jax.shard_map(
        local,
        mesh=mesh,
        in_specs=(P(None, "rows", None), P(None, None, "cols"), P("rows"), P("rows")),
        out_specs=P(None, "rows", "cols"),
        check_vma=False,
    )
```

time: 1270 us -> 637 us (0.50)
  waiting for transfers between devices: 964 us -> 275 us
  matrix products: 170 us -> 27.2 us
  Pallas kernels: 0 us -> 111 us
  blocking collectives: 40.3 us -> 122 us
  starting transfers between devices: 7.3 us -> 55.5 us
  other arithmetic: 51.7 us -> 25.4 us
  between operations: 14.1 us -> 1.28 us
    ppermute x3 -> x35, waiting for transfers between devices: 900 us -> 275 us  [the longest x20 166 us: exchange(): return lax.ppermute(value, axis, pairs)]
    dot_general x3 -> x1, matrix products: 170 us -> 27.2 us  [local(): jnp.dot(hidden_acts[example], grads, preferred_element_type=jnp.float32)]
    pallas_call x0 -> x10, Pallas kernels: none -> 111 us  [the longest x5 61.8 us: add_products(): pl.pallas_call(functools.partial(add_kernel, slots, total is None, scale...]
    all_gather x1 -> x0, waiting for transfers between devices: 63.7 us -> none  [local(): lax.all_gather(kept_acts, 'cols', axis=2, tiled=True)]
    all_gather x0 -> x1, blocking collectives: none -> 60.5 us  [local(): kept_all = lax.all_gather(kept_index, 'rows', axis=0)]
    ppermute x3 -> x35, starting transfers between devices: 7.3 us -> 55.5 us  [the longest x5 26.6 us: local(): outer = send(own, 'inner', lambda v: lax.ppermute(v, 'rows', to_inner))]
    select_n x4 -> x2, other arithmetic: 47.6 us -> 8.18 us  [local(): own = jnp.where(position & mask != 0, other - own, own + other)]
    psum x1, blocking collectives: 40.3 us -> 61.9 us  [local(): squares = lax.psum(jnp.sum(gradient * gradient), ('rows', 'cols'))]
  transfers between devices with their start and end apart: 4 -> 35, of which waited for: 4 -> 14; matrix products, arithmetic and copies ran while one was open for 2% -> 9% of each run, Pallas kernels for 0% -> 15%
where the time goes in v1:
time: 637 us; the launch traced here: 635 us
  waiting for transfers between devices  275 us (43%)
  blocking collectives  122 us (19%)
  Pallas kernels  111 us (17%)
  starting transfers between devices  55.5 us (9%)
  matrix products  27.2 us (4%)
  other arithmetic  25.4 us (4%)
  local copies, waits for them, and re-layouts  17.1 us (3%)
    ppermute x20, waiting for transfers between devices, exchange(): return lax.ppermute(value, axis, pairs)  166 us
    psum x1, blocking collectives, local(): squares = lax.psum(jnp.sum(gradient * gradient), ('rows', 'cols'))  61.9 us
    pallas_call x5, Pallas kernels, add_products(): pl.pallas_call(functools.partial(add_kernel, slots, total is None, scale...  61.8 us
    all_gather x1, blocking collectives, local(): kept_all = lax.all_gather(kept_index, 'rows', axis=0)  60.5 us
    ppermute x5, waiting for transfers between devices, local(): outer = send(own, 'inner', lambda v: lax.ppermute(v, 'rows', to_inner))  56.3 us
    ppermute x5, waiting for transfers between devices, local(): lax.ppermute(v, 'rows', to_outer)  52.8 us
    pallas_call x5, Pallas kernels, pick_all(): pl.pallas_call(functools.partial(pick_kernel, segments), out_shape=(shape...  48.8 us
    dot_general x1, matrix products, local(): jnp.dot(hidden_acts[example], grads, preferred_element_type=jnp.float32)  27.2 us
  transfers between devices with their start and end apart: 35, of which 14 were waited for; matrix products, arithmetic and copies ran while one was open for 9% of the time, Pallas kernels for 15%

profile of v1, /device:TPU:0, one launch (start us, length us, event | category | flops | bytes accessed | tf_op | source)
XLA Modules:
  0.0 634.8 jit_solution(15228057838771863390)
XLA Ops:
  0.7 1.7 convert_multiply_fusion
  2.4 3.0 collective-permute-start
  5.4 38.6 %collective-permute-done = f32[3456,128]{1,0:T(8,128)S(1)} collective-permute-done((f32[3456,128]{1,0:T(8,128)S(1)}, f32[3456,128]{1,0:T(8,128)S(1)}, u32[]{:S(2)}, u32[]{:S(2)}) %collective-permute-start) | collective-permute-done | bytes 1769504 | tf_op jit(solution)/shard_map/ppermute | solution.py:19
  44.0 4.1 add_select_fusion
  48.2 1.7 collective-permute-start.1
  49.9 38.1 %collective-permute-done.1 = f32[3456,128]{1,0:T(8,128)S(1)} collective-permute-done((f32[3456,128]{1,0:T(8,128)S(1)}, f32[3456,128]{1,0:T(8,128)S(1)}, u32[]{:S(2)}, u32[]{:S(2)}) %collective-permute-start.1) | collective-permute-done | bytes 1769504 | tf_op jit(solution)/shard_map/ppermute | solution.py:19
  89.4 37.5 %collective-permute-done.2 = f32[3456,128]{1,0:T(8,128)S(1)} collective-permute-done((f32[3456,128]{1,0:T(8,128)S(1)}, f32[3456,128]{1,0:T(8,128)S(1)}, u32[]{:S(2)}, u32[]{:S(2)}) %collective-permute-start.2) | collective-permute-done | bytes 1769504 | tf_op jit(solution)/shard_map/ppermute | solution.py:19
  128.1 3.6 collective-permute-start.5
  131.7 33.6 %collective-permute-done.3 = f32[3456,128]{1,0:T(8,128)} collective-permute-done((f32[3456,128]{1,0:T(8,128)S(1)}, f32[3456,128]{1,0:T(8,128)}, u32[]{:S(2)}, u32[]{:S(2)}) %collective-permute-start.3) | collective-permute-done | bytes 1769504 | tf_op jit(solution)/shard_map/ppermute | solution.py:19
  168.0 60.5 %all-gather = s32[16384]{0:T(1024)} all-gather(s32[2048]{0:T(1024)} %param.7), channel_id=2, replica_groups=mesh['rows'=8,'cols'=4] {'rows'}, dimensions={0}, use_global_device_ids=true | all-gather | bytes 73728 | tf_op jit(solution)/shard_map/all_gather | solution.py:211
  228.5 1.5 reshape.82
  230.0 1.6 dynamic-slice_reduce_fusion.2
  236.3 5.5 subtract_convert_fusion.table_ref
  241.8 9.9 %shard_map.50 = (f32[2,8,256,128]{3,2,1,0:T(8,128)S(1)}, f32[8,256,128]{2,1,0:T(8,128)S(1)}, f32[8,256,128]{2,1,0:T(8,128)S(1)}) custom-call(f32[2]{0:T(128)S(1)} %pad_maximum_fusion.flags_ref, f32[3456,128]{1,0:T(8,128)S(1)} %get-tuple-element.96.own_ref, f32[3456,128]{1,0:T(8,128)S(1)} %collective-permute-done.5.outer_ref, ...), custom_call_target="tpu_custom_call" | custom-call | flops 2147483648 | bytes 16121856 | tf_op jit(solution)/shard_map/pallas_call | solution.py:119
  252.6 4.1 add_select_fusion.1
  256.6 1.9 collective-permute-start.6
  258.5 28.3 %collective-permute-done.6.outer_ref = f32[3456,128]{1,0:T(8,128)S(1)} collective-permute-done((f32[3456,128]{1,0:T(8,128)S(1)}, f32[3456,128]{1,0:T(8,128)S(1)}, u32[]{:S(2)}, u32[]{:S(2)}) %collective-permute-start.6) | collective-permute-done | bytes 1769504 | tf_op jit(solution)/shard_map/ppermute | solution.py:264
  286.8 9.7 %shard_map.49 = (f32[2,8,256,128]{3,2,1,0:T(8,128)S(1)}, f32[8,256,128]{2,1,0:T(8,128)S(1)}, f32[8,256,128]{2,1,0:T(8,128)S(1)}) custom-call(f32[2]{0:T(128)S(1)} %pad_maximum_fusion.flags_ref, f32[3456,128]{1,0:T(8,128)S(1)} %get-tuple-element.53.own_ref, f32[3456,128]{1,0:T(8,128)S(1)} %collective-permute-done.6.outer_ref, ...), custom_call_target="tpu_custom_call" | custom-call | flops 2147483648 | bytes 16121856 | tf_op jit(solution)/shard_map/pallas_call | solution.py:119
  297.4 7.3 %collective-permute-start.7 = (f32[3456,128]{1,0:T(8,128)S(1)}, f32[3456,128]{1,0:T(8,128)S(1)}, u32[]{:S(2)}, u32[]{:S(2)}) collective-permute-start(f32[3456,128]{1,0:T(8,128)S(1)} %get-tuple-element.54.own_ref), channel_id=1, source_target_pairs={{0,8},{4,12},{24,16},{28,20},{1,9},{5,13},{25,17},{29,21},{2,10},{... | collective-permute-start | bytes 5308424 | tf_op jit(solution)/shard_map/ppermute | solution.py:264
  306.1 15.4 %collective-permute-done.15 = f32[8,256,128]{2,1,0:T(8,128)S(1)} collective-permute-done((f32[8,256,128]{2,1,0:T(8,128)S(1)}, f32[8,256,128]{2,1,0:T(8,128)S(1)}, u32[]{:S(2)}, u32[]{:S(2)}) %collective-permute-start.15) | collective-permute-done | bytes 1048608 | tf_op jit(solution)/shard_map/ppermute | solution.py:268
  321.7 1.9 collective-permute-start.20
  323.6 8.0 %collective-permute-done.7.outer_ref = f32[3456,128]{1,0:T(8,128)S(1)} collective-permute-done((f32[3456,128]{1,0:T(8,128)S(1)}, f32[3456,128]{1,0:T(8,128)S(1)}, u32[]{:S(2)}, u32[]{:S(2)}) %collective-permute-start.7) | collective-permute-done | bytes 1769504 | tf_op jit(solution)/shard_map/ppermute | solution.py:264
  331.5 9.7 %shard_map.48 = (f32[2,8,256,128]{3,2,1,0:T(8,128)S(1)}, f32[8,256,128]{2,1,0:T(8,128)S(1)}, f32[8,256,128]{2,1,0:T(8,128)S(1)}) custom-call(f32[2]{0:T(128)S(1)} %pad_maximum_fusion.flags_ref, f32[3456,128]{1,0:T(8,128)S(1)} %get-tuple-element.54.own_ref, f32[3456,128]{1,0:T(8,128)S(1)} %collective-permute-done.7.outer_ref, ...), custom_call_target="tpu_custom_call" | custom-call | flops 2147483648 | bytes 16121856 | tf_op jit(solution)/shard_map/pallas_call | solution.py:119
  342.1 6.2 collective-permute-start.8
  349.9 15.3 %collective-permute-done.16 = f32[8,256,128]{2,1,0:T(8,128)S(1)} collective-permute-done((f32[8,256,128]{2,1,0:T(8,128)S(1)}, f32[8,256,128]{2,1,0:T(8,128)S(1)}, u32[]{:S(2)}, u32[]{:S(2)}) %collective-permute-start.16) | collective-permute-done | bytes 1048608 | tf_op jit(solution)/shard_map/ppermute | solution.py:268
  366.6 2.2 collective-permute-start.21
  368.8 6.4 %collective-permute-done.8.outer_ref = f32[3456,128]{1,0:T(8,128)S(1)} collective-permute-done((f32[3456,128]{1,0:T(8,128)S(1)}, f32[3456,128]{1,0:T(8,128)S(1)}, u32[]{:S(2)}, u32[]{:S(2)}) %collective-permute-start.8) | collective-permute-done | bytes 1769504 | tf_op jit(solution)/shard_map/ppermute | solution.py:264
  375.2 9.7 %shard_map.47 = (f32[2,8,256,128]{3,2,1,0:T(8,128)S(1)}, f32[8,256,128]{2,1,0:T(8,128)S(1)}, f32[8,256,128]{2,1,0:T(8,128)S(1)}) custom-call(f32[2]{0:T(128)S(1)} %pad_maximum_fusion.flags_ref, f32[3456,128]{1,0:T(8,128)S(1)} %get-tuple-element.55.own_ref, f32[3456,128]{1,0:T(8,128)S(1)} %collective-permute-done.8.outer_ref, ...), custom_call_target="tpu_custom_call" | custom-call | flops 2147483648 | bytes 16121856 | tf_op jit(solution)/shard_map/pallas_call | solution.py:119
  387.2 7.6 %collective-permute-start.9 = (f32[3456,128]{1,0:T(8,128)S(1)}, f32[3456,128]{1,0:T(8,128)S(1)}, u32[]{:S(2)}, u32[]{:S(2)}) collective-permute-start(f32[3456,128]{1,0:T(8,128)S(1)} %get-tuple-element.56.own_ref), channel_id=1, source_target_pairs={{0,8},{4,12},{24,16},{28,20},{1,9},{5,13},{25,17},{29,21},{2,10},{... | collective-permute-start | bytes 5308424 | tf_op jit(solution)/shard_map/ppermute | solution.py:264
  394.9 12.0 %collective-permute-done.17 = f32[8,256,128]{2,1,0:T(8,128)S(1)} collective-permute-done((f32[8,256,128]{2,1,0:T(8,128)S(1)}, f32[8,256,128]{2,1,0:T(8,128)S(1)}, u32[]{:S(2)}, u32[]{:S(2)}) %collective-permute-start.17) | collective-permute-done | bytes 1048608 | tf_op jit(solution)/shard_map/ppermute | solution.py:268
  408.4 1.5 collective-permute-start.18
  410.0 13.6 %collective-permute-done.9.outer_ref = f32[3456,128]{1,0:T(8,128)S(1)} collective-permute-done((f32[3456,128]{1,0:T(8,128)S(1)}, f32[3456,128]{1,0:T(8,128)S(1)}, u32[]{:S(2)}, u32[]{:S(2)}) %collective-permute-start.9) | collective-permute-done | bytes 1769504 | tf_op jit(solution)/shard_map/ppermute | solution.py:264
  423.6 9.7 %shard_map.46 = (f32[2,8,256,128]{3,2,1,0:T(8,128)S(1)}, f32[8,256,128]{2,1,0:T(8,128)S(1)}, f32[8,256,128]{2,1,0:T(8,128)S(1)}) custom-call(f32[2]{0:T(128)S(1)} %pad_maximum_fusion.flags_ref, f32[3456,128]{1,0:T(8,128)S(1)} %get-tuple-element.56.own_ref, f32[3456,128]{1,0:T(8,128)S(1)} %collective-permute-done.9.outer_ref, ...), custom_call_target="tpu_custom_call" | custom-call | flops 2147483648 | bytes 16121856 | tf_op jit(solution)/shard_map/pallas_call | solution.py:119
  434.3 10.1 %collective-permute-done.18 = f32[8,256,128]{2,1,0:T(8,128)S(1)} collective-permute-done((f32[8,256,128]{2,1,0:T(8,128)}, f32[8,256,128]{2,1,0:T(8,128)S(1)}, u32[]{:S(2)}, u32[]{:S(2)}) %collective-permute-start.18) | collective-permute-done | bytes 1048608 | tf_op jit(solution)/shard_map/ppermute | solution.py:268
  445.9 2.5 collective-permute-start.23
  452.9 9.0 %collective-permute-done.23.refs_1_ = f32[2048,128]{1,0:T(8,128)} collective-permute-done((f32[2048,128]{1,0:T(8,128)S(1)}, f32[2048,128]{1,0:T(8,128)}, u32[]{:S(2)}, u32[]{:S(2)}) %collective-permute-start.23) | collective-permute-done | bytes 1048608 | tf_op jit(solution)/shard_map/ppermute | solution.py:19
  462.9 27.2 %fusion.1 = f32[]{:T(128)} fusion(bf16[1,3456,2560]{2,1,0:T(8,128)(2,1)} %param.4, bf16[1,2560,1280]{2,1,0:T(8,128)(2,1)S(1)} %bitcast.113), kind=kOutput, calls=%fused_computation.3 | convolution fusion | flops 22658088960 | bytes 24248324 | tf_op jit(solution)/shard_map/dot_general | solution.py:243
  490.1 61.9 %psum.7 = f32[]{:T(128)} all-reduce(f32[]{:T(128)} %fusion.1), channel_id=1, replica_groups=mesh['rows'=8,'cols'=4] {'rows','cols'}, use_global_device_ids=true, to_apply=%region_1.2 | all-reduce | flops 1 | bytes 8 | tf_op jit(solution)/shard_map/psum | solution.py:244
  552.7 2.2 fusion.18
  554.8 2.5 collective-permute-start.24
  557.8 2.9 copy-done
  560.7 9.0 %shard_map.51.refs_8_ = f32[2048,1280]{1,0:T(8,128)} custom-call(s32[4]{0:T(128)S(1)} %pad_add_fusion.4.places_ref, f32[2048,128]{1,0:T(8,128)S(1)} %bitcast.136, f32[2048,128]{1,0:T(8,128)S(1)} %copy-done.5, f32[2048,128]{1,0:T(8,128)S(1)} %copy-done.7, f32[2048,128]{1,0:T(8,128)S(1)} %copy-done.9, bf16[2560,1280]{1,0:T(8,128)(2,1)S(1)} %bitcast.114, ...), custom_call_target="tpu_custom_call" | custom-call | flops 5368709120 | bytes 25165824 | tf_op jit(solution)/shard_map/pallas_call | solution.py:171
  569.7 9.5 %collective-permute-done.24.refs_1_ = f32[2048,128]{1,0:T(8,128)S(1)} collective-permute-done((f32[2048,128]{1,0:T(8,128)S(1)}, f32[2048,128]{1,0:T(8,128)S(1)}, u32[]{:S(2)}, u32[]{:S(2)}) %collective-permute-start.24) | collective-permute-done | bytes 1048608 | tf_op jit(solution)/shard_map/ppermute | solution.py:19
  579.2 2.9 copy-done.1
  582.1 12.9 %shard_map.52.refs_8_ = f32[2048,1280]{1,0:T(8,128)} custom-call(s32[4]{0:T(128)S(1)} %pad_add_fusion.3.places_ref, f32[2048,128]{1,0:T(8,128)S(1)} %bitcast.142, f32[2048,128]{1,0:T(8,128)S(1)} %copy-done.12, f32[2048,128]{1,0:T(8,128)S(1)} %copy-done.14, f32[2048,128]{1,0:T(8,128)S(1)} %copy-done.16, ...), custom_call_target="tpu_custom_call", output_to_operand_aliasing={{}: (9, {})} | custom-call | flops 5368709120 | bytes 25165824 | tf_op jit(solution)/shard_map/pallas_call | solution.py:171
  595.0 12.9 %shard_map.53.refs_8_ = f32[2048,1280]{1,0:T(8,128)} custom-call(s32[4]{0:T(128)S(1)} %pad_add_fusion.2.places_ref, f32[2048,128]{1,0:T(8,128)S(1)} %bitcast.145, f32[2048,128]{1,0:T(8,128)S(1)} %copy-done.18, f32[2048,128]{1,0:T(8,128)S(1)} %copy-done.20, f32[2048,128]{1,0:T(8,128)S(1)} %copy-done.22, ...), custom_call_target="tpu_custom_call", output_to_operand_aliasing={{}: (9, {})} | custom-call | flops 5368709120 | bytes 25165824 | tf_op jit(solution)/shard_map/pallas_call | solution.py:171
  607.9 14.0 %shard_map.54.refs_8_ = f32[2048,1280]{1,0:T(8,128)} custom-call(s32[4]{0:T(128)S(1)} %pad_add_fusion.1.places_ref, f32[2048,128]{1,0:T(8,128)S(1)} %bitcast.148, f32[2048,128]{1,0:T(8,128)} %collective-permute-done.23.refs_1_, f32[2048,128]{1,0:T(8,128)S(1)} %copy-done.24, ...), custom_call_target="tpu_custom_call", output_to_operand_aliasing={{}: (9, {})} | custom-call | flops 5368709120 | bytes 25165824 | tf_op jit(solution)/shard_map/pallas_call | solution.py:171
  622.0 12.9 %shard_map.55 = f32[2048,1280]{1,0:T(8,128)} custom-call(s32[4]{0:T(128)S(1)} %pad_add_fusion.places_ref, f32[2048,128]{1,0:T(8,128)S(1)} %bitcast.139, f32[2048,128]{1,0:T(8,128)S(1)} %collective-permute-done.24.refs_1_, f32[2048,128]{1,0:T(8,128)S(1)} %collective-permute-done.33.refs_2_, ...), custom_call_target="tpu_custom_call", output_to_operand_aliasing={{}: (9, {})} | custom-call | flops 5368709120 | bytes 25165824 | tf_op jit(solution)/shard_map/pallas_call | solution.py:171
  (132 shorter events, 29.7 us)
Async XLA Ops:
  2.4 41.6 %collective-permute-start = (f32[3456,128]{1,0:T(8,128)S(1)}, f32[3456,128]{1,0:T(8,128)S(1)}, u32[]{:S(2)}, u32[]{:S(2)}) collective-permute-start(f32[3456,128]{1,0:T(8,128)S(1)} %convert_multiply_fusion), channel_id=1, source_target_pairs={{0,4},{4,0},{8,12},{12,8},{16,20},{20,16},{24,28},{28,24},{1,5},{5... | collective-permute-start | bytes 5308424 | tf_op jit(solution)/shard_map/ppermute | solution.py:19
  48.2 39.8 %collective-permute-start.1 = (f32[3456,128]{1,0:T(8,128)S(1)}, f32[3456,128]{1,0:T(8,128)S(1)}, u32[]{:S(2)}, u32[]{:S(2)}) collective-permute-start(f32[3456,128]{1,0:T(8,128)S(1)} %get-tuple-element.49), channel_id=1, source_target_pairs={{0,4},{4,0},{8,12},{12,8},{16,20},{20,16},{24,28},{28,24},{1,5},{5... | collective-permute-start | bytes 5308424 | tf_op jit(solution)/shard_map/ppermute | solution.py:19
  87.9 40.2 %copy-start.28 = (f32[3456,128]{1,0:T(8,128)}, f32[3456,128]{1,0:T(8,128)S(1)}, u32[]{:S(2)}) copy-start(f32[3456,128]{1,0:T(8,128)S(1)} %collective-permute-done.1) | copy-start | bytes 5308420
  87.9 38.9 %collective-permute-start.2 = (f32[3456,128]{1,0:T(8,128)S(1)}, f32[3456,128]{1,0:T(8,128)S(1)}, u32[]{:S(2)}, u32[]{:S(2)}) collective-permute-start(f32[3456,128]{1,0:T(8,128)S(1)} %get-tuple-element.50), channel_id=1, source_target_pairs={{0,4},{4,0},{8,12},{12,8},{16,20},{20,16},{24,28},{28,24},{1,5},{5... | collective-permute-start | bytes 5308424 | tf_op jit(solution)/shard_map/ppermute | solution.py:19
  126.8 38.6 %collective-permute-start.3 = (f32[3456,128]{1,0:T(8,128)S(1)}, f32[3456,128]{1,0:T(8,128)}, u32[]{:S(2)}, u32[]{:S(2)}) collective-permute-start(f32[3456,128]{1,0:T(8,128)S(1)} %get-tuple-element.51), channel_id=1, source_target_pairs={{0,4},{4,0},{8,12},{12,8},{16,20},{20,16},{24,28},{28,24},{1,5},{5... | collective-permute-start | bytes 5308424 | tf_op jit(solution)/shard_map/ppermute | solution.py:19
  128.1 113.7 %collective-permute-start.5 = (f32[3456,128]{1,0:T(8,128)S(1)}, f32[3456,128]{1,0:T(8,128)S(1)}, u32[]{:S(2)}, u32[]{:S(2)}) collective-permute-start(f32[3456,128]{1,0:T(8,128)S(1)} %get-tuple-element.96.own_ref), channel_id=1, source_target_pairs={{0,8},{4,12},{24,16},{28,20},{1,9},{5,13},{25,17},{29,21},{2,10},{... | collective-permute-start | bytes 5308424 | tf_op jit(solution)/shard_map/ppermute | solution.py:264
  165.4 87.1 %collective-permute-start.4 = (f32[3456,128]{1,0:T(8,128)}, f32[3456,128]{1,0:T(8,128)}, u32[]{:S(2)}, u32[]{:S(2)}) collective-permute-start(f32[3456,128]{1,0:T(8,128)} %get-tuple-element.52), channel_id=1, source_target_pairs={{0,4},{4,0},{8,12},{12,8},{16,20},{20,16},{24,28},{28,24},{1,5},{5... | collective-permute-start | bytes 5308424 | tf_op jit(solution)/shard_map/ppermute | solution.py:19
  251.7 44.8 %collective-permute-start.10 = (f32[2,8,256,128]{3,2,1,0:T(8,128)S(1)}, f32[2,8,256,128]{3,2,1,0:T(8,128)S(1)}, u32[]{:S(2)}, u32[]{:S(2)}) collective-permute-start(f32[2,8,256,128]{3,2,1,0:T(8,128)S(1)} %get-tuple-element.62), channel_id=1, source_target_pairs={{8,16},{12,20},{16,8},{20,12},{9,17},{13,21},{17,9},{21,13},{10,18... | collective-permute-start | bytes 6291464 | tf_op jit(solution)/shard_map/ppermute | solution.py:266
  256.6 30.2 %collective-permute-start.6 = (f32[3456,128]{1,0:T(8,128)S(1)}, f32[3456,128]{1,0:T(8,128)S(1)}, u32[]{:S(2)}, u32[]{:S(2)}) collective-permute-start(f32[3456,128]{1,0:T(8,128)S(1)} %get-tuple-element.53.own_ref), channel_id=1, source_target_pairs={{0,8},{4,12},{24,16},{28,20},{1,9},{5,13},{25,17},{29,21},{2,10},{... | collective-permute-start | bytes 5308424 | tf_op jit(solution)/shard_map/ppermute | solution.py:264
  296.6 44.7 %collective-permute-start.11 = (f32[2,8,256,128]{3,2,1,0:T(8,128)S(1)}, f32[2,8,256,128]{3,2,1,0:T(8,128)S(1)}, u32[]{:S(2)}, u32[]{:S(2)}) collective-permute-start(f32[2,8,256,128]{3,2,1,0:T(8,128)S(1)} %get-tuple-element.63), channel_id=1, source_target_pairs={{8,16},{12,20},{16,8},{20,12},{9,17},{13,21},{17,9},{21,13},{10,18... | collective-permute-start | bytes 6291464 | tf_op jit(solution)/shard_map/ppermute | solution.py:266
  297.4 34.2 %collective-permute-start.7 = (f32[3456,128]{1,0:T(8,128)S(1)}, f32[3456,128]{1,0:T(8,128)S(1)}, u32[]{:S(2)}, u32[]{:S(2)}) collective-permute-start(f32[3456,128]{1,0:T(8,128)S(1)} %get-tuple-element.54.own_ref), channel_id=1, source_target_pairs={{0,8},{4,12},{24,16},{28,20},{1,9},{5,13},{25,17},{29,21},{2,10},{... | collective-permute-start | bytes 5308424 | tf_op jit(solution)/shard_map/ppermute | solution.py:264
  304.8 16.7 %collective-permute-start.15 = (f32[8,256,128]{2,1,0:T(8,128)S(1)}, f32[8,256,128]{2,1,0:T(8,128)S(1)}, u32[]{:S(2)}, u32[]{:S(2)}) collective-permute-start(f32[8,256,128]{2,1,0:T(8,128)S(1)} %fusion.12), channel_id=1, source_target_pairs={{8,0},{12,4},{16,24},{20,28},{9,1},{13,5},{17,25},{21,29},{10,2},{... | collective-permute-start | bytes 3145736 | tf_op jit(solution)/shard_map/ppermute | solution.py:268
  321.7 28.1 %collective-permute-start.20 = (f32[2048,128]{1,0:T(8,128)S(1)}, f32[2048,128]{1,0:T(8,128)S(1)}, u32[]{:S(2)}, u32[]{:S(2)}) collective-permute-start(f32[2048,128]{1,0:T(8,128)S(1)} %bitcast.134), channel_id=1, source_target_pairs={{0,2},{1,3},{2,0},{3,1},{4,6},{5,7},{6,4},{7,5},{8,10},{9,11},{10,... | collective-permute-start | bytes 3145736 | tf_op jit(solution)/shard_map/ppermute | solution.py:19
  323.6 26.2 %collective-permute-start.25 = (f32[2048,128]{1,0:T(8,128)S(1)}, f32[2048,128]{1,0:T(8,128)S(1)}, u32[]{:S(2)}, u32[]{:S(2)}) collective-permute-start(f32[2048,128]{1,0:T(8,128)S(1)} %bitcast.135), channel_id=1, source_target_pairs={{0,1},{1,0},{2,3},{3,2},{4,5},{5,4},{6,7},{7,6},{8,9},{9,8},{10,11... | collective-permute-start | bytes 3145736 | tf_op jit(solution)/shard_map/ppermute | solution.py:19
  341.3 23.9 %copy-start.27 = (f32[2,8,256,128]{3,2,1,0:T(8,128)}, f32[2,8,256,128]{3,2,1,0:T(8,128)S(1)}, u32[]{:S(2)}) copy-start(f32[2,8,256,128]{3,2,1,0:T(8,128)S(1)} %collective-permute-done.11) | copy-start | bytes 6291460
  341.3 43.7 %collective-permute-start.12 = (f32[2,8,256,128]{3,2,1,0:T(8,128)S(1)}, f32[2,8,256,128]{3,2,1,0:T(8,128)S(1)}, u32[]{:S(2)}, u32[]{:S(2)}) collective-permute-start(f32[2,8,256,128]{3,2,1,0:T(8,128)S(1)} %get-tuple-element.64), channel_id=1, source_target_pairs={{8,16},{12,20},{16,8},{20,12},{9,17},{13,21},{17,9},{21,13},{10,18... | collective-permute-start | bytes 6291464 | tf_op jit(solution)/shard_map/ppermute | solution.py:266
  342.1 33.1 %collective-permute-start.8 = (f32[3456,128]{1,0:T(8,128)S(1)}, f32[3456,128]{1,0:T(8,128)S(1)}, u32[]{:S(2)}, u32[]{:S(2)}) collective-permute-start(f32[3456,128]{1,0:T(8,128)S(1)} %get-tuple-element.55.own_ref), channel_id=1, source_target_pairs={{0,8},{4,12},{24,16},{28,20},{1,9},{5,13},{25,17},{29,21},{2,10},{... | collective-permute-start | bytes 5308424 | tf_op jit(solution)/shard_map/ppermute | solution.py:264
  348.5 16.7 %collective-permute-start.16 = (f32[8,256,128]{2,1,0:T(8,128)S(1)}, f32[8,256,128]{2,1,0:T(8,128)S(1)}, u32[]{:S(2)}, u32[]{:S(2)}) collective-permute-start(f32[8,256,128]{2,1,0:T(8,128)S(1)} %fusion.13), channel_id=1, source_target_pairs={{8,0},{12,4},{16,24},{20,28},{9,1},{13,5},{17,25},{21,29},{10,2},{... | collective-permute-start | bytes 3145736 | tf_op jit(solution)/shard_map/ppermute | solution.py:268
  349.8 16.8 %copy-start.4 = (f32[2048,128]{1,0:T(8,128)}, f32[2048,128]{1,0:T(8,128)S(1)}, u32[]{:S(2)}) copy-start(f32[2048,128]{1,0:T(8,128)S(1)} %collective-permute-done.20.refs_1_) | copy-start | bytes 3145732
  349.8 16.8 %copy-start.6 = (f32[2048,128]{1,0:T(8,128)}, f32[2048,128]{1,0:T(8,128)S(1)}, u32[]{:S(2)}) copy-start(f32[2048,128]{1,0:T(8,128)S(1)} %collective-permute-done.25.refs_2_) | copy-start | bytes 3145732
  349.8 19.0 %collective-permute-start.26 = (f32[2048,128]{1,0:T(8,128)S(1)}, f32[2048,128]{1,0:T(8,128)S(1)}, u32[]{:S(2)}, u32[]{:S(2)}) collective-permute-start(f32[2048,128]{1,0:T(8,128)S(1)} %collective-permute-done.20.refs_1_), channel_id=1, source_target_pairs={{0,1},{1,0},{2,3},{3,2},{4,5},{5,4},{6,7},{7,6},{8,9},{9,8},{10,11... | collective-permute-start | bytes 3145736 | tf_op jit(solution)/shard_map/ppermute | solution.py:19
  366.6 28.2 %collective-permute-start.21 = (f32[2048,128]{1,0:T(8,128)S(1)}, f32[2048,128]{1,0:T(8,128)S(1)}, u32[]{:S(2)}, u32[]{:S(2)}) collective-permute-start(f32[2048,128]{1,0:T(8,128)S(1)} %bitcast.140), channel_id=1, source_target_pairs={{0,2},{1,3},{2,0},{3,1},{4,6},{5,7},{6,4},{7,5},{8,10},{9,11},{10,... | collective-permute-start | bytes 3145736 | tf_op jit(solution)/shard_map/ppermute | solution.py:19
  368.8 16.2 %copy-start.8 = (f32[2048,128]{1,0:T(8,128)}, f32[2048,128]{1,0:T(8,128)S(1)}, u32[]{:S(2)}) copy-start(f32[2048,128]{1,0:T(8,128)S(1)} %collective-permute-done.26.refs_3_) | copy-start | bytes 3145732
  368.8 26.1 %collective-permute-start.27 = (f32[2048,128]{1,0:T(8,128)S(1)}, f32[2048,128]{1,0:T(8,128)S(1)}, u32[]{:S(2)}, u32[]{:S(2)}) collective-permute-start(f32[2048,128]{1,0:T(8,128)S(1)} %bitcast.141), channel_id=1, source_target_pairs={{0,1},{1,0},{2,3},{3,2},{4,5},{5,4},{6,7},{7,6},{8,9},{9,8},{10,11... | collective-permute-start | bytes 3145736 | tf_op jit(solution)/shard_map/ppermute | solution.py:19
  385.0 22.3 %collective-permute-start.13 = (f32[2,8,256,128]{3,2,1,0:T(8,128)S(1)}, f32[2,8,256,128]{3,2,1,0:T(8,128)S(1)}, u32[]{:S(2)}, u32[]{:S(2)}) collective-permute-start(f32[2,8,256,128]{3,2,1,0:T(8,128)S(1)} %get-tuple-element.65), channel_id=1, source_target_pairs={{8,16},{12,20},{16,8},{20,12},{9,17},{13,21},{17,9},{21,13},{10,18... | collective-permute-start | bytes 6291464 | tf_op jit(solution)/shard_map/ppermute | solution.py:266
  385.9 21.0 %collective-permute-start.17 = (f32[8,256,128]{2,1,0:T(8,128)S(1)}, f32[8,256,128]{2,1,0:T(8,128)S(1)}, u32[]{:S(2)}, u32[]{:S(2)}) collective-permute-start(f32[8,256,128]{2,1,0:T(8,128)S(1)} %fusion.14), channel_id=1, source_target_pairs={{8,0},{12,4},{16,24},{20,28},{9,1},{13,5},{17,25},{21,29},{10,2},{... | collective-permute-start | bytes 3145736 | tf_op jit(solution)/shard_map/ppermute | solution.py:268
  387.2 36.4 %collective-permute-start.9 = (f32[3456,128]{1,0:T(8,128)S(1)}, f32[3456,128]{1,0:T(8,128)S(1)}, u32[]{:S(2)}, u32[]{:S(2)}) collective-permute-start(f32[3456,128]{1,0:T(8,128)S(1)} %get-tuple-element.56.own_ref), channel_id=1, source_target_pairs={{0,8},{4,12},{24,16},{28,20},{1,9},{5,13},{25,17},{29,21},{2,10},{... | collective-permute-start | bytes 5308424 | tf_op jit(solution)/shard_map/ppermute | solution.py:264
  394.9 12.4 %collective-permute-start.28 = (f32[2048,128]{1,0:T(8,128)S(1)}, f32[2048,128]{1,0:T(8,128)S(1)}, u32[]{:S(2)}, u32[]{:S(2)}) collective-permute-start(f32[2048,128]{1,0:T(8,128)S(1)} %collective-permute-done.21.refs_1_), channel_id=1, source_target_pairs={{0,1},{1,0},{2,3},{3,2},{4,5},{5,4},{6,7},{7,6},{8,9},{9,8},{10,11... | collective-permute-start | bytes 3145736 | tf_op jit(solution)/shard_map/ppermute | solution.py:19
  407.1 27.1 %collective-permute-start.22 = (f32[2048,128]{1,0:T(8,128)S(1)}, f32[2048,128]{1,0:T(8,128)S(1)}, u32[]{:S(2)}, u32[]{:S(2)}) collective-permute-start(f32[2048,128]{1,0:T(8,128)S(1)} %bitcast.143), channel_id=1, source_target_pairs={{0,2},{1,3},{2,0},{3,1},{4,6},{5,7},{6,4},{7,5},{8,10},{9,11},{10,... | collective-permute-start | bytes 3145736 | tf_op jit(solution)/shard_map/ppermute | solution.py:19
  407.3 26.9 %collective-permute-start.29 = (f32[2048,128]{1,0:T(8,128)S(1)}, f32[2048,128]{1,0:T(8,128)S(1)}, u32[]{:S(2)}, u32[]{:S(2)}) collective-permute-start(f32[2048,128]{1,0:T(8,128)S(1)} %bitcast.144), channel_id=1, source_target_pairs={{0,1},{1,0},{2,3},{3,2},{4,5},{5,4},{6,7},{7,6},{8,9},{9,8},{10,11... | collective-permute-start | bytes 3145736 | tf_op jit(solution)/shard_map/ppermute | solution.py:19
  407.3 55.6 %slice-start = ((s8[6553600]{0:T(1024)(128)(4,1)}), s8[4194304]{0:T(1024)(128)(4,1)S(1)}, s32[]{:S(2)}) async-start(s8[6553600]{0:T(1024)(128)(4,1)} %bitcast.112), calls=%async_computation | async-start | bytes 8388608
  408.4 54.5 %slice-start.1 = ((s8[6553600]{0:T(1024)(128)(4,1)}), s8[2359296]{0:T(1024)(128)(4,1)S(1)}, s32[]{:S(2)}) async-start(s8[6553600]{0:T(1024)(128)(4,1)} %bitcast.112), calls=%async_computation.1 | async-start | bytes 4718592
  408.4 36.0 %collective-permute-start.18 = (f32[8,256,128]{2,1,0:T(8,128)}, f32[8,256,128]{2,1,0:T(8,128)S(1)}, u32[]{:S(2)}, u32[]{:S(2)}) collective-permute-start(f32[8,256,128]{2,1,0:T(8,128)} %fusion.15), channel_id=1, source_target_pairs={{8,0},{12,4},{16,24},{20,28},{9,1},{13,5},{17,25},{21,29},{10,2},{... | collective-permute-start | bytes 3145736 | tf_op jit(solution)/shard_map/ppermute | solution.py:268
  433.4 17.0 %collective-permute-start.14 = (f32[2,8,256,128]{3,2,1,0:T(8,128)S(1)}, f32[2,8,256,128]{3,2,1,0:T(8,128)S(1)}, u32[]{:S(2)}, u32[]{:S(2)}) collective-permute-start(f32[2,8,256,128]{3,2,1,0:T(8,128)S(1)} %get-tuple-element.66), channel_id=1, source_target_pairs={{8,16},{12,20},{16,8},{20,12},{9,17},{13,21},{17,9},{21,13},{10,18... | collective-permute-start | bytes 6291464 | tf_op jit(solution)/shard_map/ppermute | solution.py:266
  434.2 14.2 %collective-permute-start.30 = (f32[2048,128]{1,0:T(8,128)S(1)}, f32[2048,128]{1,0:T(8,128)S(1)}, u32[]{:S(2)}, u32[]{:S(2)}) collective-permute-start(f32[2048,128]{1,0:T(8,128)S(1)} %collective-permute-done.22.refs_1_), channel_id=1, source_target_pairs={{0,1},{1,0},{2,3},{3,2},{4,5},{5,4},{6,7},{7,6},{8,9},{9,8},{10,11... | collective-permute-start | bytes 3145736 | tf_op jit(solution)/shard_map/ppermute | solution.py:19
  445.9 16.1 %collective-permute-start.23 = (f32[2048,128]{1,0:T(8,128)S(1)}, f32[2048,128]{1,0:T(8,128)}, u32[]{:S(2)}, u32[]{:S(2)}) collective-permute-start(f32[2048,128]{1,0:T(8,128)S(1)} %bitcast.146), channel_id=1, source_target_pairs={{0,2},{1,3},{2,0},{3,1},{4,6},{5,7},{6,4},{7,5},{8,10},{9,11},{10,... | collective-permute-start | bytes 3145736 | tf_op jit(solution)/shard_map/ppermute | solution.py:19
  449.4 12.6 %collective-permute-start.31 = (f32[2048,128]{1,0:T(8,128)S(1)}, f32[2048,128]{1,0:T(8,128)S(1)}, u32[]{:S(2)}, u32[]{:S(2)}) collective-permute-start(f32[2048,128]{1,0:T(8,128)S(1)} %bitcast.147), channel_id=1, source_target_pairs={{0,1},{1,0},{2,3},{3,2},{4,5},{5,4},{6,7},{7,6},{8,9},{9,8},{10,11... | collective-permute-start | bytes 3145736 | tf_op jit(solution)/shard_map/ppermute | solution.py:19
  451.6 101.0 %collective-permute-start.19 = (f32[8,256,128]{2,1,0:T(8,128)}, f32[8,256,128]{2,1,0:T(8,128)}, u32[]{:S(2)}, u32[]{:S(2)}) collective-permute-start(f32[8,256,128]{2,1,0:T(8,128)} %fusion.16), channel_id=1, source_target_pairs={{8,0},{12,4},{16,24},{20,28},{9,1},{13,5},{17,25},{21,29},{10,2},{... | collective-permute-start | bytes 3145736 | tf_op jit(solution)/shard_map/ppermute | solution.py:268
  462.9 94.5 %collective-permute-start.32 = (f32[2048,128]{1,0:T(8,128)}, f32[2048,128]{1,0:T(8,128)}, u32[]{:S(2)}, u32[]{:S(2)}) collective-permute-start(f32[2048,128]{1,0:T(8,128)} %collective-permute-done.23.refs_1_), channel_id=1, source_target_pairs={{0,1},{1,0},{2,3},{3,2},{4,5},{5,4},{6,7},{7,6},{8,9},{9,8},{10,11... | collective-permute-start | bytes 3145736 | tf_op jit(solution)/shard_map/ppermute | solution.py:19
  554.8 24.3 %collective-permute-start.24 = (f32[2048,128]{1,0:T(8,128)S(1)}, f32[2048,128]{1,0:T(8,128)S(1)}, u32[]{:S(2)}, u32[]{:S(2)}) collective-permute-start(f32[2048,128]{1,0:T(8,128)S(1)} %bitcast.137), channel_id=1, source_target_pairs={{0,2},{1,3},{2,0},{3,1},{4,6},{5,7},{6,4},{7,5},{8,10},{9,11},{10,... | collective-permute-start | bytes 3145736 | tf_op jit(solution)/shard_map/ppermute | solution.py:19
  557.4 21.8 %collective-permute-start.33 = (f32[2048,128]{1,0:T(8,128)S(1)}, f32[2048,128]{1,0:T(8,128)S(1)}, u32[]{:S(2)}, u32[]{:S(2)}) collective-permute-start(f32[2048,128]{1,0:T(8,128)S(1)} %bitcast.138), channel_id=1, source_target_pairs={{0,1},{1,0},{2,3},{3,2},{4,5},{5,4},{6,7},{7,6},{8,9},{9,8},{10,11... | collective-permute-start | bytes 3145736 | tf_op jit(solution)/shard_map/ppermute | solution.py:19
  560.6 18.5 %copy-start.12 = (f32[2048,128]{1,0:T(8,128)S(1)}, f32[2048,128]{1,0:T(8,128)}, u32[]{:S(2)}) copy-start(f32[2048,128]{1,0:T(8,128)} %copy-done.11) | copy-start | bytes 3145732
  560.6 18.5 %copy-start.14 = (f32[2048,128]{1,0:T(8,128)S(1)}, f32[2048,128]{1,0:T(8,128)}, u32[]{:S(2)}) copy-start(f32[2048,128]{1,0:T(8,128)} %copy-done.13) | copy-start | bytes 3145732
  560.6 18.6 %copy-start.16 = (f32[2048,128]{1,0:T(8,128)S(1)}, f32[2048,128]{1,0:T(8,128)}, u32[]{:S(2)}) copy-start(f32[2048,128]{1,0:T(8,128)} %copy-done.15) | copy-start | bytes 3145732
  560.6 34.3 %copy-start.18 = (f32[2048,128]{1,0:T(8,128)S(1)}, f32[2048,128]{1,0:T(8,128)}, u32[]{:S(2)}) copy-start(f32[2048,128]{1,0:T(8,128)} %copy-done.17) | copy-start | bytes 3145732
  560.6 34.3 %copy-start.20 = (f32[2048,128]{1,0:T(8,128)S(1)}, f32[2048,128]{1,0:T(8,128)}, u32[]{:S(2)}) copy-start(f32[2048,128]{1,0:T(8,128)} %copy-done.19) | copy-start | bytes 3145732
  560.7 34.3 %copy-start.22 = (f32[2048,128]{1,0:T(8,128)S(1)}, f32[2048,128]{1,0:T(8,128)}, u32[]{:S(2)}) copy-start(f32[2048,128]{1,0:T(8,128)} %copy-done.21) | copy-start | bytes 3145732
  579.2 42.8 %collective-permute-start.34 = (f32[2048,128]{1,0:T(8,128)S(1)}, f32[2048,128]{1,0:T(8,128)S(1)}, u32[]{:S(2)}, u32[]{:S(2)}) collective-permute-start(f32[2048,128]{1,0:T(8,128)S(1)} %collective-permute-done.24.refs_1_), channel_id=1, source_target_pairs={{0,1},{1,0},{2,3},{3,2},{4,5},{5,4},{6,7},{7,6},{8,9},{9,8},{10,11... | collective-permute-start | bytes 3145736 | tf_op jit(solution)/shard_map/ppermute | solution.py:19
  (21 other events, 150.0 us)

commit v2 on v1

--- a/solution.py
+++ b/solution.py
@@ -208,20 +208,17 @@
     inner = (line == 1) | (line == 2)
     left = line < 2
 
-    kept_all = lax.all_gather(kept_index, "rows", axis=0)
-
-    def kept_of(group):
-        whole = lax.dynamic_index_in_dim(kept_all, group * low + offset, 0, keepdims=False)
-        return whole.reshape(row_devices, keep // row_devices)
-
+    kept_of = lambda step: exchange(kept_index, "rows", step * low).reshape(
+        row_devices, keep // row_devices
+    )
     own_kept = kept_index.reshape(row_devices, keep // row_devices)
     tables = table(
         jnp.stack(
             [
-                kept_of(jnp.where(left, 2, 1)),
-                kept_of(jnp.where(left, 3, 0)),
+                kept_of(3),
+                kept_of(2),
                 own_kept,
-                kept_of(jnp.where(left, 0, 3)),
+                kept_of(1),
             ]
         ),
         length,
@@ -241,7 +238,13 @@
     for example in range(examples):
         grads = out_grads[example]
         gradient = jnp.dot(hidden_acts[example], grads, preferred_element_type=jnp.float32)
-        squares = lax.psum(jnp.sum(gradient * gradient), ("rows", "cols"))
+        squares = jnp.sum(gradient * gradient).reshape(1)
+        part = squares
+        for axis, size in (("rows", row_devices), ("cols", col_devices)):
+            mask = 1
+            while mask < size:
+                squares = squares + exchange(squares, axis, mask)
+                mask *= 2
         inv_norm = lax.rsqrt(squares / D + epsilon)
         total = None
         done = {}
@@ -251,19 +254,40 @@
             done[name] = arrived
             return arrived
 
-        for number in range(block):
+        def mix(number, ready):
             acts = lax.dynamic_slice_in_dim(
                 hidden_acts[example], column * share + number * chunk, chunk, 1
             )
-            own = acts.astype(jnp.float32) * signs
+            own = after(acts.astype(jnp.float32) * signs, ready)
             mask = 1
             while mask < low:
                 other = send(own, ("mix", mask), lambda v: exchange(v, "rows", mask))
-                own = jnp.where((position & mask) != 0, other - own, own + other)
-                mask *= 2
-            outer = send(own, "inner", lambda v: lax.ppermute(v, "rows", to_inner))
+                if mask * 2 < low:
+                    own = jnp.where((position & mask) != 0, other - own, own + other)
+                    mask *= 2
+                    continue
+                upper = (position & mask) != 0
+                return lambda v: jnp.where(upper, v[0] - v[1], v[1] + v[0]), (other, own)
+            return lambda v: v[1], (own, own)
+
+        join, pair = mix(0, None)
+        pair, _ = lax.optimization_barrier((pair, part))
+        own = join(pair)
+        across_sums = []
+        for number in range(block):
+            outer = lax.ppermute(own, "rows", to_inner)
+            if number + 1 < block:
+                join, pair = mix(number + 1, own)
+                waits = [tables] if number == 0 else []
+                if number >= 2:
+                    waits.append(across_sums[number - 2])
+                if number == block - 2:
+                    waits.append(squares)
+                pair, outer, own, *_ = lax.optimization_barrier((pair, outer, own, *waits))
+                following = join(pair)
             far, here, near = pick_all(tables, own, outer, side, inner, pad_rows)
             arrived = send(far, "across", lambda v: lax.ppermute(v, "rows", across))
+            across_sums.append(arrived)
             last = send(
                 arrived[1] + near, "outer", lambda v: lax.ppermute(v, "rows", to_outer)
             )
@@ -272,14 +296,18 @@
             order = [0]
             mask = col_devices // 2
             while mask:
+                sent = [after(v, total) for v in slots[1:]]
                 slots += [
-                    send(v, ("cols", mask), lambda v: exchange(v, "cols", mask)) for v in slots
+                    send(v, ("cols", mask), lambda v: exchange(v, "cols", mask))
+                    for v in [slots[0], *sent]
                 ]
                 order += [slot ^ mask for slot in order]
                 mask //= 2
             places = jnp.stack([(column ^ slot) * block + number for slot in order])
             scale = inv_norm if number == block - 1 else None
             total = add_products(total, slots, grads, places, scale)
+            if number + 1 < block:
+                own = following
         results.append(total)
     return jnp.stack(results)
 

time: 637 us -> 483 us (0.76)
  blocking collectives: 122 us -> 0 us
  waiting for transfers between devices: 275 us -> 205 us
  local copies, waits for them, and re-layouts: 17.1 us -> 29 us
  other arithmetic: 25.4 us -> 35.6 us
  Pallas kernels: 111 us -> 119 us
    psum x1 -> x0, blocking collectives: 61.9 us -> none  [local(): squares = lax.psum(jnp.sum(gradient * gradient), ('rows', 'cols'))]
    all_gather x1 -> x0, blocking collectives: 60.5 us -> none  [local(): kept_all = lax.all_gather(kept_index, 'rows', axis=0)]
    ppermute x5, waiting for transfers between devices: 56.3 us -> 1.42 us  [local(): outer = lax.ppermute(own, 'rows', to_inner)]
    ppermute x20 -> x28, waiting for transfers between devices: 166 us -> 119 us  [exchange(): return lax.ppermute(value, axis, pairs)]
    ppermute x5, waiting for transfers between devices: 52.8 us -> 85 us  [local(): lax.ppermute(v, 'rows', to_outer)]
    unnamed x68 -> x86, local copies, waits for them, and re-layouts: 8.77 us -> 24.4 us
    ppermute x20 -> x28, starting transfers between devices: 18.3 us -> 27.1 us  [exchange(): return lax.ppermute(value, axis, pairs)]
    ppermute x5, starting transfers between devices: 26.6 us -> 18.7 us  [local(): outer = lax.ppermute(own, 'rows', to_inner)]
  transfers between devices with their start and end apart: 35 -> 43, of which waited for: 14 -> 17; matrix products, arithmetic and copies ran while one was open for 9% -> 12% of each run, Pallas kernels for 15% -> 22%
where the time goes in v2:
time: 483 us; the launch traced here: 481 us
  waiting for transfers between devices  205 us (42%)
  Pallas kernels  119 us (25%)
  starting transfers between devices  60.5 us (13%)
  other arithmetic  35.6 us (7%)
  local copies, waits for them, and re-layouts  29 us (6%)
  matrix products  27.2 us (6%)
    ppermute x28, waiting for transfers between devices, exchange(): return lax.ppermute(value, axis, pairs)  119 us
    ppermute x5, waiting for transfers between devices, local(): lax.ppermute(v, 'rows', to_outer)  85 us
    pallas_call x5, Pallas kernels, add_products(): pl.pallas_call(functools.partial(add_kernel, slots, total is None, scale...  65.2 us
    pallas_call x5, Pallas kernels, pick_all(): pl.pallas_call(functools.partial(pick_kernel, segments), out_shape=(shape...  53.7 us
    dot_general x1, matrix products, local(): jnp.dot(hidden_acts[example], grads, preferred_element_type=jnp.float32)  27.2 us
    ppermute x28, starting transfers between devices, exchange(): return lax.ppermute(value, axis, pairs)  27.1 us
    unnamed x86, local copies, waits for them, and re-layouts  24.4 us
    ppermute x5, starting transfers between devices, local(): outer = lax.ppermute(own, 'rows', to_inner)  18.7 us
  transfers between devices with their start and end apart: 43, of which 17 were waited for; matrix products, arithmetic and copies ran while one was open for 12% of the time, Pallas kernels for 22%

profile of v2, /device:TPU:0, one launch (start us, length us, event | category | flops | bytes accessed | tf_op | source)
XLA Modules:
  0.0 480.9 jit_solution(6578242381849153115)
XLA Ops:
  0.7 5.8 %convert_multiply_fusion = (f32[3456,128]{1,0:T(8,128)S(1)}, f32[3456,128]{1,0:T(8,128)}, f32[3456,128]{1,0:T(8,128)}, f32[3456,128]{1,0:T(8,128)}, f32[3456,128]{1,0:T(8,128)}) fusion(bf16[1,3456,2560]{2,1,0:T(8,128)(2,1)} %param.4, s32[]{:T(128)S(6)} %select_n.79, f32[3456]{0:T(1024)S(1)} %convert_element_type.43, s32[]{:T(128)S(6)} %select_n.78, ...), kind=kLoop, calls=%fused_computation.4 | loop fusion | flops 4423680 | bytes 13284884 | tf_op jit(solution)/shard_map/mul | solution.py:261
  6.5 2.9 collective-permute-start
  9.4 27.2 %fusion.1 = f32[]{:T(128)} fusion(bf16[1,3456,2560]{2,1,0:T(8,128)(2,1)} %param.4, bf16[1,2560,1280]{2,1,0:T(8,128)(2,1)S(1)} %copy-done), kind=kOutput, calls=%fused_computation.3 | convolution fusion | flops 22658088960 | bytes 24248324 | tf_op jit(solution)/shard_map/dot_general | solution.py:240
  36.7 11.4 %collective-permute-done = f32[3456,128]{1,0:T(8,128)S(1)} collective-permute-done((f32[3456,128]{1,0:T(8,128)S(1)}, f32[3456,128]{1,0:T(8,128)S(1)}, u32[]{:S(2)}, u32[]{:S(2)}) %collective-permute-start) | collective-permute-done | bytes 1769504 | tf_op jit(solution)/shard_map/ppermute | solution.py:19
  49.2 1.7 add_select_fusion.4.own_ref
  51.0 1.8 collective-permute-start.1
  52.8 3.6 collective-permute-start.2
  56.5 3.0 collective-permute-start.4
  61.6 31.7 %collective-permute-done.5 = s32[2048]{0:T(1024)} collective-permute-done((s32[2048]{0:T(1024)}, s32[2048]{0:T(1024)}, u32[]{:S(2)}, u32[]{:S(2)}) %collective-permute-start.5) | collective-permute-done | bytes 8224 | tf_op jit(solution)/shard_map/ppermute | solution.py:19
  98.6 5.6 %subtract_convert_fusion.table_ref = bf16[4,8,256,512]{3,2,1,0:T(8,128)(2,1)} fusion(s32[4,8,256]{2,1,0:T(8,128)S(1)} %add_and_fusion), kind=kLoop, calls=%fused_computation.2 | loop fusion | flops 25165824 | bytes 8421376 | tf_op jit(solution)/shard_map/convert_element_type | solution.py:48
  105.4 2.2 add_select_fusion.3.own_ref
  108.2 5.1 %collective-permute-start.7 = (f32[3456,128]{1,0:T(8,128)S(1)}, f32[3456,128]{1,0:T(8,128)}, u32[]{:S(2)}, u32[]{:S(2)}) collective-permute-start(f32[3456,128]{1,0:T(8,128)S(1)} %add_select_fusion.3.own_ref), channel_id=1, source_target_pairs={{0,8},{4,12},{24,16},{28,20},{1,9},{5,13},{25,17},{29,21},{2,10},{... | collective-permute-start | bytes 5308424 | tf_op jit(solution)/shard_map/ppermute | solution.py:278
  114.8 9.7 %shard_map.46 = (f32[2,8,256,128]{3,2,1,0:T(8,128)S(1)}, f32[8,256,128]{2,1,0:T(8,128)S(1)}, f32[8,256,128]{2,1,0:T(8,128)S(1)}) custom-call(f32[2]{0:T(128)S(1)} %pad_maximum_fusion.flags_ref, f32[3456,128]{1,0:T(8,128)S(1)} %add_select_fusion.4.own_ref, f32[3456,128]{1,0:T(8,128)S(1)} %copy-done.11, bf16[4,8,256,512]{3,2,1,0:T(8,128)(2,1)} %subtract_convert_fusion.table_ref), custom_call_target="tpu_custom_call" | custom-call | flops 2147483648 | bytes 16121856 | tf_op jit(solution)/shard_map/pallas_call | solution.py:119
  125.5 20.5 %collective-permute-done.6 = f32[3456,128]{1,0:T(8,128)} collective-permute-done((f32[3456,128]{1,0:T(8,128)}, f32[3456,128]{1,0:T(8,128)}, u32[]{:S(2)}, u32[]{:S(2)}) %collective-permute-start.6) | collective-permute-done | bytes 1769504 | tf_op jit(solution)/shard_map/ppermute | solution.py:19
  147.4 2.2 add_select_fusion.2.own_ref
  151.0 4.6 collective-permute-start.9
  157.0 10.3 %shard_map.47 = (f32[2,8,256,128]{3,2,1,0:T(8,128)S(1)}, f32[8,256,128]{2,1,0:T(8,128)S(1)}, f32[8,256,128]{2,1,0:T(8,128)S(1)}) custom-call(f32[2]{0:T(128)S(1)} %pad_maximum_fusion.flags_ref, f32[3456,128]{1,0:T(8,128)S(1)} %add_select_fusion.3.own_ref, f32[3456,128]{1,0:T(8,128)} %collective-permute-done.7.outer_ref, ...), custom_call_target="tpu_custom_call" | custom-call | flops 2147483648 | bytes 16121856 | tf_op jit(solution)/shard_map/pallas_call | solution.py:119
  168.1 22.6 %collective-permute-done.23 = f32[8,256,128]{2,1,0:T(8,128)S(1)} collective-permute-done((f32[8,256,128]{2,1,0:T(8,128)S(1)}, f32[8,256,128]{2,1,0:T(8,128)S(1)}, u32[]{:S(2)}, u32[]{:S(2)}) %collective-permute-start.23) | collective-permute-done | bytes 1048608 | tf_op jit(solution)/shard_map/ppermute | solution.py:292
  198.3 13.6 %collective-permute-done.28.refs_1_ = f32[2048,128]{1,0:T(8,128)} collective-permute-done((f32[2048,128]{1,0:T(8,128)S(1)}, f32[2048,128]{1,0:T(8,128)}, u32[]{:S(2)}, u32[]{:S(2)}) %collective-permute-start.28) | collective-permute-done | bytes 1048608 | tf_op jit(solution)/shard_map/ppermute | solution.py:19
  213.1 21.0 %collective-permute-done.14 = f32[1]{0:T(128)} collective-permute-done((f32[1]{0:T(128)}, f32[1]{0:T(128)}, u32[]{:S(2)}, u32[]{:S(2)}) %collective-permute-start.14) | collective-permute-done | bytes 36 | tf_op jit(solution)/shard_map/ppermute | solution.py:19
  235.4 1.8 collective-permute-start.15
  237.2 11.7 %collective-permute-done.15 = f32[1]{0:T(128)} collective-permute-done((f32[1]{0:T(128)}, f32[1]{0:T(128)}, u32[]{:S(2)}, u32[]{:S(2)}) %collective-permute-start.15) | collective-permute-done | bytes 36 | tf_op jit(solution)/shard_map/ppermute | solution.py:19
  249.6 1.9 collective-permute-start.16
  251.5 2.5 collective-permute-done.16
  256.6 2.9 collective-permute-start.18
  259.5 10.9 %shard_map.50 = (f32[2,8,256,128]{3,2,1,0:T(8,128)}, f32[8,256,128]{2,1,0:T(8,128)S(1)}, f32[8,256,128]{2,1,0:T(8,128)S(1)}) custom-call(f32[2]{0:T(128)S(1)} %pad_maximum_fusion.flags_ref, f32[3456,128]{1,0:T(8,128)S(1)} %add_select_fusion.2.own_ref, f32[3456,128]{1,0:T(8,128)S(1)} %collective-permute-done.9.outer_ref, ...), custom_call_target="tpu_custom_call" | custom-call | flops 2147483648 | bytes 16121856 | tf_op jit(solution)/shard_map/pallas_call | solution.py:119
  272.4 2.1 collective-permute-start.20
  275.2 2.0 fusion.7
  279.0 2.3 add_select_fusion.own_ref
  281.4 3.9 collective-permute-start.19
  286.8 11.0 %shard_map.49 = (f32[2,8,256,128]{3,2,1,0:T(8,128)}, f32[8,256,128]{2,1,0:T(8,128)S(1)}, f32[8,256,128]{2,1,0:T(8,128)S(1)}) custom-call(f32[2]{0:T(128)S(1)} %pad_maximum_fusion.flags_ref, f32[3456,128]{1,0:T(8,128)S(1)} %add_select_fusion.1.own_ref, f32[3456,128]{1,0:T(8,128)S(1)} %copy-done.9, bf16[4,8,256,512]{3,2,1,0:T(8,128)(2,1)} %subtract_convert_fusion.table_ref), custom_call_target="tpu_custom_call" | custom-call | flops 2147483648 | bytes 16121856 | tf_op jit(solution)/shard_map/pallas_call | solution.py:119
  299.7 2.1 collective-permute-start.21
  301.8 2.4 fusion.14
  305.6 11.0 %shard_map.51.refs_8_ = f32[2048,1280]{1,0:T(8,128)} custom-call(s32[4]{0:T(128)S(1)} %pad_add_fusion.2.places_ref, f32[2048,128]{1,0:T(8,128)S(1)} %bitcast.128, f32[2048,128]{1,0:T(8,128)} %collective-permute-done.28.refs_1_, f32[2048,128]{1,0:T(8,128)S(1)} %copy-done.13, f32[2048,128]{1,0:T(8,128)} %collective-permute-done.34.refs_3_, ...), custom_call_target="tpu_custom_call" | custom-call | flops 5368709120 | bytes 25165824 | tf_op jit(solution)/shard_map/pallas_call | solution.py:171
  317.8 32.3 %collective-permute-done.25 = f32[8,256,128]{2,1,0:T(8,128)} collective-permute-done((f32[8,256,128]{2,1,0:T(8,128)}, f32[8,256,128]{2,1,0:T(8,128)}, u32[]{:S(2)}, u32[]{:S(2)}) %collective-permute-start.25) | collective-permute-done | bytes 1048608 | tf_op jit(solution)/shard_map/ppermute | solution.py:292
  350.0 2.0 fusion.9
  352.7 11.7 %shard_map.48 = (f32[2,8,256,128]{3,2,1,0:T(8,128)}, f32[8,256,128]{2,1,0:T(8,128)S(1)}, f32[8,256,128]{2,1,0:T(8,128)S(1)}) custom-call(f32[2]{0:T(128)S(1)} %pad_maximum_fusion.flags_ref, f32[3456,128]{1,0:T(8,128)S(1)} %add_select_fusion.own_ref, f32[3456,128]{1,0:T(8,128)} %collective-permute-done.19.outer_ref, ...), custom_call_target="tpu_custom_call" | custom-call | flops 2147483648 | bytes 16121856 | tf_op jit(solution)/shard_map/pallas_call | solution.py:119
  365.4 2.1 collective-permute-start.22
  370.4 14.0 %shard_map.52.refs_8_ = f32[2048,1280]{1,0:T(8,128)} custom-call(s32[4]{0:T(128)S(1)} %pad_add_fusion.3.places_ref, f32[2048,128]{1,0:T(8,128)S(1)} %bitcast.134, f32[2048,128]{1,0:T(8,128)} %collective-permute-done.29.refs_1_, f32[2048,128]{1,0:T(8,128)S(1)} %copy-done.27, ...), custom_call_target="tpu_custom_call", output_to_operand_aliasing={{}: (9, {})} | custom-call | flops 5368709120 | bytes 25165824 | tf_op jit(solution)/shard_map/pallas_call | solution.py:171
  385.0 11.5 %collective-permute-done.26 = f32[8,256,128]{2,1,0:T(8,128)S(1)} collective-permute-done((f32[8,256,128]{2,1,0:T(8,128)S(1)}, f32[8,256,128]{2,1,0:T(8,128)S(1)}, u32[]{:S(2)}, u32[]{:S(2)}) %collective-permute-start.26) | collective-permute-done | bytes 1048608 | tf_op jit(solution)/shard_map/ppermute | solution.py:292
  403.6 2.9 copy-done.1
  406.4 13.0 %shard_map.53.refs_8_ = f32[2048,1280]{1,0:T(8,128)} custom-call(s32[4]{0:T(128)S(1)} %pad_add_fusion.1.places_ref, f32[2048,128]{1,0:T(8,128)S(1)} %bitcast.137, f32[2048,128]{1,0:T(8,128)S(1)} %copy-done.29, f32[2048,128]{1,0:T(8,128)S(1)} %copy-done.31, f32[2048,128]{1,0:T(8,128)S(1)} %copy-done.33, ...), custom_call_target="tpu_custom_call", output_to_operand_aliasing={{}: (9, {})} | custom-call | flops 5368709120 | bytes 25165824 | tf_op jit(solution)/shard_map/pallas_call | solution.py:171
  421.0 18.7 %collective-permute-done.27 = f32[8,256,128]{2,1,0:T(8,128)S(1)} collective-permute-done((f32[8,256,128]{2,1,0:T(8,128)S(1)}, f32[8,256,128]{2,1,0:T(8,128)S(1)}, u32[]{:S(2)}, u32[]{:S(2)}) %collective-permute-start.27) | collective-permute-done | bytes 1048608 | tf_op jit(solution)/shard_map/ppermute | solution.py:292
  442.7 2.9 copy-done.2
  446.8 14.0 %shard_map.54.refs_8_ = f32[2048,1280]{1,0:T(8,128)} custom-call(s32[4]{0:T(128)S(1)} %pad_add_fusion.4.places_ref, f32[2048,128]{1,0:T(8,128)S(1)} %bitcast.140, f32[2048,128]{1,0:T(8,128)} %collective-permute-done.31.refs_1_, f32[2048,128]{1,0:T(8,128)} %collective-permute-done.39.refs_2_, ...), custom_call_target="tpu_custom_call", output_to_operand_aliasing={{}: (9, {})} | custom-call | flops 5368709120 | bytes 25165824 | tf_op jit(solution)/shard_map/pallas_call | solution.py:171
  462.3 2.5 collective-permute-done.42.refs_3_
  464.9 2.9 copy-done.3
  467.7 13.2 %shard_map.55 = f32[2048,1280]{1,0:T(8,128)} custom-call(s32[4]{0:T(128)S(1)} %pad_add_fusion.places_ref, f32[2048,128]{1,0:T(8,128)S(1)} %bitcast.131, f32[2048,128]{1,0:T(8,128)S(1)} %collective-permute-done.32.refs_1_, f32[2048,128]{1,0:T(8,128)} %collective-permute-done.41.refs_2_, ...), custom_call_target="tpu_custom_call", output_to_operand_aliasing={{}: (9, {})} | custom-call | flops 5368709120 | bytes 25165824 | tf_op jit(solution)/shard_map/pallas_call | solution.py:171
  (166 shorter events, 57.9 us)
Async XLA Ops:
  6.5 41.5 %collective-permute-start = (f32[3456,128]{1,0:T(8,128)S(1)}, f32[3456,128]{1,0:T(8,128)S(1)}, u32[]{:S(2)}, u32[]{:S(2)}) collective-permute-start(f32[3456,128]{1,0:T(8,128)S(1)} %get-tuple-element.72), channel_id=1, source_target_pairs={{0,4},{4,0},{8,12},{12,8},{16,20},{20,16},{24,28},{28,24},{1,5},{5... | collective-permute-start | bytes 5308424 | tf_op jit(solution)/shard_map/ppermute | solution.py:19
  51.0 53.2 %collective-permute-start.1 = (f32[3456,128]{1,0:T(8,128)}, f32[3456,128]{1,0:T(8,128)}, u32[]{:S(2)}, u32[]{:S(2)}) collective-permute-start(f32[3456,128]{1,0:T(8,128)} %get-tuple-element.76), channel_id=1, source_target_pairs={{0,4},{4,0},{8,12},{12,8},{16,20},{20,16},{24,28},{28,24},{1,5},{5... | collective-permute-start | bytes 5308424 | tf_op jit(solution)/shard_map/ppermute | solution.py:19
  52.8 51.4 %collective-permute-start.2 = (f32[3456,128]{1,0:T(8,128)S(1)}, f32[3456,128]{1,0:T(8,128)S(1)}, u32[]{:S(2)}, u32[]{:S(2)}) collective-permute-start(f32[3456,128]{1,0:T(8,128)S(1)} %add_select_fusion.4.own_ref), channel_id=1, source_target_pairs={{0,8},{4,12},{24,16},{28,20},{1,9},{5,13},{25,17},{29,21},{2,10},{... | collective-permute-start | bytes 5308424 | tf_op jit(solution)/shard_map/ppermute | solution.py:278
  56.4 36.9 %collective-permute-start.5 = (s32[2048]{0:T(1024)}, s32[2048]{0:T(1024)}, u32[]{:S(2)}, u32[]{:S(2)}) collective-permute-start(s32[2048]{0:T(1024)} %param.7), channel_id=1, source_target_pairs={{0,8},{4,12},{8,0},{12,4},{16,24},{20,28},{24,16},{28,20},{1,9},{5... | collective-permute-start | bytes 24584 | tf_op jit(solution)/shard_map/ppermute | solution.py:19
  56.5 38.1 %collective-permute-start.4 = (s32[2048]{0:T(1024)}, s32[2048]{0:T(1024)}, u32[]{:S(2)}, u32[]{:S(2)}) collective-permute-start(s32[2048]{0:T(1024)} %param.7), channel_id=1, source_target_pairs={{0,16},{4,20},{8,24},{12,28},{16,0},{20,4},{24,8},{28,12},{1,17},{... | collective-permute-start | bytes 24584 | tf_op jit(solution)/shard_map/ppermute | solution.py:19
  59.5 37.0 %collective-permute-start.3 = (s32[2048]{0:T(1024)}, s32[2048]{0:T(1024)}, u32[]{:S(2)}, u32[]{:S(2)}) collective-permute-start(s32[2048]{0:T(1024)} %param.7), channel_id=1, source_target_pairs={{0,24},{4,28},{8,16},{12,20},{16,8},{20,12},{24,0},{28,4},{1,25},{... | collective-permute-start | bytes 24584 | tf_op jit(solution)/shard_map/ppermute | solution.py:19
  107.6 38.4 %collective-permute-start.6 = (f32[3456,128]{1,0:T(8,128)}, f32[3456,128]{1,0:T(8,128)}, u32[]{:S(2)}, u32[]{:S(2)}) collective-permute-start(f32[3456,128]{1,0:T(8,128)} %get-tuple-element.80), channel_id=1, source_target_pairs={{0,4},{4,0},{8,12},{12,8},{16,20},{20,16},{24,28},{28,24},{1,5},{5... | collective-permute-start | bytes 5308424 | tf_op jit(solution)/shard_map/ppermute | solution.py:19
  108.2 39.2 %collective-permute-start.7 = (f32[3456,128]{1,0:T(8,128)S(1)}, f32[3456,128]{1,0:T(8,128)}, u32[]{:S(2)}, u32[]{:S(2)}) collective-permute-start(f32[3456,128]{1,0:T(8,128)S(1)} %add_select_fusion.3.own_ref), channel_id=1, source_target_pairs={{0,8},{4,12},{24,16},{28,20},{1,9},{5,13},{25,17},{29,21},{2,10},{... | collective-permute-start | bytes 5308424 | tf_op jit(solution)/shard_map/ppermute | solution.py:278
  124.5 31.1 %collective-permute-start.10 = (f32[2,8,256,128]{3,2,1,0:T(8,128)S(1)}, f32[2,8,256,128]{3,2,1,0:T(8,128)S(1)}, u32[]{:S(2)}, u32[]{:S(2)}) collective-permute-start(f32[2,8,256,128]{3,2,1,0:T(8,128)S(1)} %get-tuple-element.85), channel_id=1, source_target_pairs={{8,16},{12,20},{16,8},{20,12},{9,17},{13,21},{17,9},{21,13},{10,18... | collective-permute-start | bytes 6291464 | tf_op jit(solution)/shard_map/ppermute | solution.py:289
  149.6 42.9 %collective-permute-start.8 = (f32[3456,128]{1,0:T(8,128)S(1)}, f32[3456,128]{1,0:T(8,128)S(1)}, u32[]{:S(2)}, u32[]{:S(2)}) collective-permute-start(f32[3456,128]{1,0:T(8,128)S(1)} %copy-done.36), channel_id=1, source_target_pairs={{0,4},{4,0},{8,12},{12,8},{16,20},{20,16},{24,28},{28,24},{1,5},{5... | collective-permute-start | bytes 5308424 | tf_op jit(solution)/shard_map/ppermute | solution.py:19
  151.0 41.5 %collective-permute-start.9 = (f32[3456,128]{1,0:T(8,128)S(1)}, f32[3456,128]{1,0:T(8,128)S(1)}, u32[]{:S(2)}, u32[]{:S(2)}) collective-permute-start(f32[3456,128]{1,0:T(8,128)S(1)} %add_select_fusion.2.own_ref), channel_id=1, source_target_pairs={{0,8},{4,12},{24,16},{28,20},{1,9},{5,13},{25,17},{29,21},{2,10},{... | collective-permute-start | bytes 5308424 | tf_op jit(solution)/shard_map/ppermute | solution.py:278
  155.7 35.0 %collective-permute-start.23 = (f32[8,256,128]{2,1,0:T(8,128)S(1)}, f32[8,256,128]{2,1,0:T(8,128)S(1)}, u32[]{:S(2)}, u32[]{:S(2)}) collective-permute-start(f32[8,256,128]{2,1,0:T(8,128)S(1)} %fusion.12), channel_id=1, source_target_pairs={{8,0},{12,4},{16,24},{20,28},{9,1},{13,5},{17,25},{21,29},{10,2},{... | collective-permute-start | bytes 3145736 | tf_op jit(solution)/shard_map/ppermute | solution.py:292
  167.3 28.2 %collective-permute-start.13 = (f32[2,8,256,128]{3,2,1,0:T(8,128)S(1)}, f32[2,8,256,128]{3,2,1,0:T(8,128)S(1)}, u32[]{:S(2)}, u32[]{:S(2)}) collective-permute-start(f32[2,8,256,128]{3,2,1,0:T(8,128)S(1)} %get-tuple-element.93), channel_id=1, source_target_pairs={{8,16},{12,20},{16,8},{20,12},{9,17},{13,21},{17,9},{21,13},{10,18... | collective-permute-start | bytes 6291464 | tf_op jit(solution)/shard_map/ppermute | solution.py:289
  190.9 21.0 %collective-permute-start.28 = (f32[2048,128]{1,0:T(8,128)S(1)}, f32[2048,128]{1,0:T(8,128)}, u32[]{:S(2)}, u32[]{:S(2)}) collective-permute-start(f32[2048,128]{1,0:T(8,128)S(1)} %bitcast.126), channel_id=1, source_target_pairs={{0,2},{1,3},{2,0},{3,1},{4,6},{5,7},{6,4},{7,5},{8,10},{9,11},{10,... | collective-permute-start | bytes 3145736 | tf_op jit(solution)/shard_map/ppermute | solution.py:19
  192.5 19.4 %collective-permute-start.33 = (f32[2048,128]{1,0:T(8,128)S(1)}, f32[2048,128]{1,0:T(8,128)S(1)}, u32[]{:S(2)}, u32[]{:S(2)}) collective-permute-start(f32[2048,128]{1,0:T(8,128)S(1)} %bitcast.127), channel_id=1, source_target_pairs={{0,1},{1,0},{2,3},{3,2},{4,5},{5,4},{6,7},{7,6},{8,9},{9,8},{10,11... | collective-permute-start | bytes 3145736 | tf_op jit(solution)/shard_map/ppermute | solution.py:19
  192.7 85.1 %collective-permute-start.11 = (f32[3456,128]{1,0:T(8,128)}, f32[3456,128]{1,0:T(8,128)}, u32[]{:S(2)}, u32[]{:S(2)}) collective-permute-start(f32[3456,128]{1,0:T(8,128)} %get-tuple-element.95), channel_id=1, source_target_pairs={{0,4},{4,0},{8,12},{12,8},{16,20},{20,16},{24,28},{28,24},{1,5},{5... | collective-permute-start | bytes 5308424 | tf_op jit(solution)/shard_map/ppermute | solution.py:19
  194.0 83.8 %collective-permute-start.12 = (f32[3456,128]{1,0:T(8,128)S(1)}, f32[3456,128]{1,0:T(8,128)S(1)}, u32[]{:S(2)}, u32[]{:S(2)}) collective-permute-start(f32[3456,128]{1,0:T(8,128)S(1)} %add_select_fusion.1.own_ref), channel_id=1, source_target_pairs={{0,8},{4,12},{24,16},{28,20},{1,9},{5,13},{25,17},{29,21},{2,10},{... | collective-permute-start | bytes 5308424 | tf_op jit(solution)/shard_map/ppermute | solution.py:278
  195.6 74.8 %copy-start.37 = (f32[2,8,256,128]{3,2,1,0:T(8,128)}, f32[2,8,256,128]{3,2,1,0:T(8,128)S(1)}, u32[]{:S(2)}) copy-start(f32[2,8,256,128]{3,2,1,0:T(8,128)S(1)} %collective-permute-done.13) | copy-start | bytes 6291460
  196.8 78.4 %collective-permute-start.24 = (f32[8,256,128]{2,1,0:T(8,128)}, f32[8,256,128]{2,1,0:T(8,128)}, u32[]{:S(2)}, u32[]{:S(2)}) collective-permute-start(f32[8,256,128]{2,1,0:T(8,128)} %fusion.13), channel_id=1, source_target_pairs={{8,0},{12,4},{16,24},{20,28},{9,1},{13,5},{17,25},{21,29},{10,2},{... | collective-permute-start | bytes 3145736 | tf_op jit(solution)/shard_map/ppermute | solution.py:292
  211.9 58.5 %copy-start.12 = (f32[2048,128]{1,0:T(8,128)}, f32[2048,128]{1,0:T(8,128)S(1)}, u32[]{:S(2)}) copy-start(f32[2048,128]{1,0:T(8,128)S(1)} %collective-permute-done.33.refs_2_) | copy-start | bytes 3145732
  211.9 65.9 %collective-permute-start.34 = (f32[2048,128]{1,0:T(8,128)}, f32[2048,128]{1,0:T(8,128)}, u32[]{:S(2)}, u32[]{:S(2)}) collective-permute-start(f32[2048,128]{1,0:T(8,128)} %collective-permute-done.28.refs_1_), channel_id=1, source_target_pairs={{0,1},{1,0},{2,3},{3,2},{4,5},{5,4},{6,7},{7,6},{8,9},{9,8},{10,11... | collective-permute-start | bytes 3145736 | tf_op jit(solution)/shard_map/ppermute | solution.py:19
  211.9 22.2 %collective-permute-start.14 = (f32[1]{0:T(128)}, f32[1]{0:T(128)}, u32[]{:S(2)}, u32[]{:S(2)}) collective-permute-start(f32[1]{0:T(128)} %bitcast.13), channel_id=1, source_target_pairs={{0,4},{4,0},{8,12},{12,8},{16,20},{20,16},{24,28},{28,24},{1,5},{5... | collective-permute-start | bytes 20 | tf_op jit(solution)/shard_map/ppermute | solution.py:19
  235.4 13.5 %collective-permute-start.15 = (f32[1]{0:T(128)}, f32[1]{0:T(128)}, u32[]{:S(2)}, u32[]{:S(2)}) collective-permute-start(f32[1]{0:T(128)} %add.164), channel_id=1, source_target_pairs={{0,8},{4,12},{8,0},{12,4},{16,24},{20,28},{24,16},{28,20},{1,9},{5... | collective-permute-start | bytes 20 | tf_op jit(solution)/shard_map/ppermute | solution.py:19
  249.6 4.5 collective-permute-start.16
  254.7 1.3 collective-permute-start.17
  256.6 15.8 %collective-permute-start.18 = (f32[1]{0:T(128)}, f32[1]{0:T(128)}, u32[]{:S(2)}, u32[]{:S(2)}) collective-permute-start(f32[1]{0:T(128)} %add.167), channel_id=1, source_target_pairs={{0,2},{1,3},{2,0},{3,1},{4,6},{5,7},{6,4},{7,5},{8,10},{9,11},{10,... | collective-permute-start | bytes 20 | tf_op jit(solution)/shard_map/ppermute | solution.py:19
  272.4 27.3 %collective-permute-start.20 = (f32[2,8,256,128]{3,2,1,0:T(8,128)}, f32[2,8,256,128]{3,2,1,0:T(8,128)}, u32[]{:S(2)}, u32[]{:S(2)}) collective-permute-start(f32[2,8,256,128]{3,2,1,0:T(8,128)} %get-tuple-element.104), channel_id=1, source_target_pairs={{8,16},{12,20},{16,8},{20,12},{9,17},{13,21},{17,9},{21,13},{10,18... | collective-permute-start | bytes 6291464 | tf_op jit(solution)/shard_map/ppermute | solution.py:289
  277.2 39.3 %collective-permute-start.29 = (f32[2048,128]{1,0:T(8,128)S(1)}, f32[2048,128]{1,0:T(8,128)}, u32[]{:S(2)}, u32[]{:S(2)}) collective-permute-start(f32[2048,128]{1,0:T(8,128)S(1)} %bitcast.132), channel_id=1, source_target_pairs={{0,2},{1,3},{2,0},{3,1},{4,6},{5,7},{6,4},{7,5},{8,10},{9,11},{10,... | collective-permute-start | bytes 3145736 | tf_op jit(solution)/shard_map/ppermute | solution.py:19
  277.8 38.8 %collective-permute-start.35 = (f32[2048,128]{1,0:T(8,128)S(1)}, f32[2048,128]{1,0:T(8,128)S(1)}, u32[]{:S(2)}, u32[]{:S(2)}) collective-permute-start(f32[2048,128]{1,0:T(8,128)S(1)} %bitcast.133), channel_id=1, source_target_pairs={{0,1},{1,0},{2,3},{3,2},{4,5},{5,4},{6,7},{7,6},{8,9},{9,8},{10,11... | collective-permute-start | bytes 3145736 | tf_op jit(solution)/shard_map/ppermute | solution.py:19
  279.0 26.5 %slice-start = ((s8[6553600]{0:T(1024)(128)(4,1)}), s8[4194304]{0:T(1024)(128)(4,1)S(1)}, s32[]{:S(2)}) async-start(s8[6553600]{0:T(1024)(128)(4,1)} %bitcast.102), calls=%async_computation | async-start | bytes 8388608
  281.4 71.3 %collective-permute-start.19 = (f32[3456,128]{1,0:T(8,128)S(1)}, f32[3456,128]{1,0:T(8,128)}, u32[]{:S(2)}, u32[]{:S(2)}) collective-permute-start(f32[3456,128]{1,0:T(8,128)S(1)} %add_select_fusion.own_ref), channel_id=1, source_target_pairs={{0,8},{4,12},{24,16},{28,20},{1,9},{5,13},{25,17},{29,21},{2,10},{... | collective-permute-start | bytes 5308424 | tf_op jit(solution)/shard_map/ppermute | solution.py:278
  299.7 65.7 %collective-permute-start.21 = (f32[2,8,256,128]{3,2,1,0:T(8,128)}, f32[2,8,256,128]{3,2,1,0:T(8,128)}, u32[]{:S(2)}, u32[]{:S(2)}) collective-permute-start(f32[2,8,256,128]{3,2,1,0:T(8,128)} %get-tuple-element.105), channel_id=1, source_target_pairs={{8,16},{12,20},{16,8},{20,12},{9,17},{13,21},{17,9},{21,13},{10,18... | collective-permute-start | bytes 6291464 | tf_op jit(solution)/shard_map/ppermute | solution.py:289
  304.2 45.8 %collective-permute-start.25 = (f32[8,256,128]{2,1,0:T(8,128)}, f32[8,256,128]{2,1,0:T(8,128)}, u32[]{:S(2)}, u32[]{:S(2)}) collective-permute-start(f32[8,256,128]{2,1,0:T(8,128)} %fusion.14), channel_id=1, source_target_pairs={{8,0},{12,4},{16,24},{20,28},{9,1},{13,5},{17,25},{21,29},{10,2},{... | collective-permute-start | bytes 3145736 | tf_op jit(solution)/shard_map/ppermute | solution.py:292
  317.5 35.1 %collective-permute-start.36 = (f32[2048,128]{1,0:T(8,128)}, f32[2048,128]{1,0:T(8,128)}, u32[]{:S(2)}, u32[]{:S(2)}) collective-permute-start(f32[2048,128]{1,0:T(8,128)} %collective-permute-done.29.refs_1_), channel_id=1, source_target_pairs={{0,1},{1,0},{2,3},{3,2},{4,5},{5,4},{6,7},{7,6},{8,9},{9,8},{10,11... | collective-permute-start | bytes 3145736 | tf_op jit(solution)/shard_map/ppermute | solution.py:19
  352.0 32.3 %collective-permute-start.30 = (f32[2048,128]{1,0:T(8,128)S(1)}, f32[2048,128]{1,0:T(8,128)S(1)}, u32[]{:S(2)}, u32[]{:S(2)}) collective-permute-start(f32[2048,128]{1,0:T(8,128)S(1)} %bitcast.135), channel_id=1, source_target_pairs={{0,2},{1,3},{2,0},{3,1},{4,6},{5,7},{6,4},{7,5},{8,10},{9,11},{10,... | collective-permute-start | bytes 3145736 | tf_op jit(solution)/shard_map/ppermute | solution.py:19
  352.6 31.8 %collective-permute-start.37 = (f32[2048,128]{1,0:T(8,128)S(1)}, f32[2048,128]{1,0:T(8,128)S(1)}, u32[]{:S(2)}, u32[]{:S(2)}) collective-permute-start(f32[2048,128]{1,0:T(8,128)S(1)} %bitcast.136), channel_id=1, source_target_pairs={{0,1},{1,0},{2,3},{3,2},{4,5},{5,4},{6,7},{7,6},{8,9},{9,8},{10,11... | collective-permute-start | bytes 3145736 | tf_op jit(solution)/shard_map/ppermute | solution.py:19
  365.4 35.2 %collective-permute-start.22 = (f32[2,8,256,128]{3,2,1,0:T(8,128)}, f32[2,8,256,128]{3,2,1,0:T(8,128)}, u32[]{:S(2)}, u32[]{:S(2)}) collective-permute-start(f32[2,8,256,128]{3,2,1,0:T(8,128)} %get-tuple-element.106), channel_id=1, source_target_pairs={{8,16},{12,20},{16,8},{20,12},{9,17},{13,21},{17,9},{21,13},{10,18... | collective-permute-start | bytes 6291464 | tf_op jit(solution)/shard_map/ppermute | solution.py:289
  368.9 27.6 %copy-start.16 = (f32[8,256,128]{2,1,0:T(8,128)S(1)}, f32[8,256,128]{2,1,0:T(8,128)}, u32[]{:S(2)}) copy-start(f32[8,256,128]{2,1,0:T(8,128)} %copy-done.15) | copy-start | bytes 3145732
  368.9 27.6 %collective-permute-start.26 = (f32[8,256,128]{2,1,0:T(8,128)S(1)}, f32[8,256,128]{2,1,0:T(8,128)S(1)}, u32[]{:S(2)}, u32[]{:S(2)}) collective-permute-start(f32[8,256,128]{2,1,0:T(8,128)S(1)} %fusion.15), channel_id=1, source_target_pairs={{8,0},{12,4},{16,24},{20,28},{9,1},{13,5},{17,25},{21,29},{10,2},{... | collective-permute-start | bytes 3145736 | tf_op jit(solution)/shard_map/ppermute | solution.py:292
  384.4 15.2 %collective-permute-start.38 = (f32[2048,128]{1,0:T(8,128)S(1)}, f32[2048,128]{1,0:T(8,128)S(1)}, u32[]{:S(2)}, u32[]{:S(2)}) collective-permute-start(f32[2048,128]{1,0:T(8,128)S(1)} %collective-permute-done.30.refs_1_), channel_id=1, source_target_pairs={{0,1},{1,0},{2,3},{3,2},{4,5},{5,4},{6,7},{7,6},{8,9},{9,8},{10,11... | collective-permute-start | bytes 3145736 | tf_op jit(solution)/shard_map/ppermute | solution.py:19
  398.0 23.0 %collective-permute-start.31 = (f32[2048,128]{1,0:T(8,128)S(1)}, f32[2048,128]{1,0:T(8,128)}, u32[]{:S(2)}, u32[]{:S(2)}) collective-permute-start(f32[2048,128]{1,0:T(8,128)S(1)} %bitcast.138), channel_id=1, source_target_pairs={{0,2},{1,3},{2,0},{3,1},{4,6},{5,7},{6,4},{7,5},{8,10},{9,11},{10,... | collective-permute-start | bytes 3145736 | tf_op jit(solution)/shard_map/ppermute | solution.py:19
  400.6 20.4 %collective-permute-start.39 = (f32[2048,128]{1,0:T(8,128)S(1)}, f32[2048,128]{1,0:T(8,128)}, u32[]{:S(2)}, u32[]{:S(2)}) collective-permute-start(f32[2048,128]{1,0:T(8,128)S(1)} %bitcast.139), channel_id=1, source_target_pairs={{0,1},{1,0},{2,3},{3,2},{4,5},{5,4},{6,7},{7,6},{8,9},{9,8},{10,11... | collective-permute-start | bytes 3145736 | tf_op jit(solution)/shard_map/ppermute | solution.py:19
  402.2 37.5 %collective-permute-start.27 = (f32[8,256,128]{2,1,0:T(8,128)S(1)}, f32[8,256,128]{2,1,0:T(8,128)S(1)}, u32[]{:S(2)}, u32[]{:S(2)}) collective-permute-start(f32[8,256,128]{2,1,0:T(8,128)S(1)} %fusion.16), channel_id=1, source_target_pairs={{8,0},{12,4},{16,24},{20,28},{9,1},{13,5},{17,25},{21,29},{10,2},{... | collective-permute-start | bytes 3145736 | tf_op jit(solution)/shard_map/ppermute | solution.py:292
  406.4 33.3 %copy-start.19 = (f32[8,256,128]{2,1,0:T(8,128)S(1)}, f32[8,256,128]{2,1,0:T(8,128)}, u32[]{:S(2)}) copy-start(f32[8,256,128]{2,1,0:T(8,128)} %copy-done.18) | copy-start | bytes 3145732
  421.0 20.6 %collective-permute-start.40 = (f32[2048,128]{1,0:T(8,128)}, f32[2048,128]{1,0:T(8,128)S(1)}, u32[]{:S(2)}, u32[]{:S(2)}) collective-permute-start(f32[2048,128]{1,0:T(8,128)} %collective-permute-done.31.refs_1_), channel_id=1, source_target_pairs={{0,1},{1,0},{2,3},{3,2},{4,5},{5,4},{6,7},{7,6},{8,9},{9,8},{10,11... | collective-permute-start | bytes 3145736 | tf_op jit(solution)/shard_map/ppermute | solution.py:19
  441.1 21.1 %collective-permute-start.32 = (f32[2048,128]{1,0:T(8,128)S(1)}, f32[2048,128]{1,0:T(8,128)S(1)}, u32[]{:S(2)}, u32[]{:S(2)}) collective-permute-start(f32[2048,128]{1,0:T(8,128)S(1)} %bitcast.129), channel_id=1, source_target_pairs={{0,2},{1,3},{2,0},{3,1},{4,6},{5,7},{6,4},{7,5},{8,10},{9,11},{10,... | collective-permute-start | bytes 3145736 | tf_op jit(solution)/shard_map/ppermute | solution.py:19
  442.6 19.5 %collective-permute-start.41 = (f32[2048,128]{1,0:T(8,128)S(1)}, f32[2048,128]{1,0:T(8,128)}, u32[]{:S(2)}, u32[]{:S(2)}) collective-permute-start(f32[2048,128]{1,0:T(8,128)S(1)} %bitcast.130), channel_id=1, source_target_pairs={{0,1},{1,0},{2,3},{3,2},{4,5},{5,4},{6,7},{7,6},{8,9},{9,8},{10,11... | collective-permute-start | bytes 3145736 | tf_op jit(solution)/shard_map/ppermute | solution.py:19
  462.2 2.7 collective-permute-start.42
  (38 other events, 242.0 us)
